TPU v7x, 32 devices: a whole 2x2x4 slice. The times are simulated.
32 devices in a mesh: replica: 4 (over z), tensor: 8 (over y, x, core).
Axes of the slice: x: 2, y: 2, z: 4, core: 2. Of those that a mesh axis runs over, the one named last changes fastest.
Arguments:
- hidden_input: bfloat16 [640, 2, 8192], P('replica', None, 'tensor'), may hold values from -200 to 200
- input_norm_gain: bfloat16 [8192], replicated, may hold values from 0.099609375 to 1.8984375
- merged_weight: bfloat16 [8192, 6144], P(None, 'tensor'), may hold values from -0.0625 to 0.0625
- output_weight: bfloat16 [4096, 8192], P('tensor'), may hold values from -0.375 to 0.375
- adapter_down: bfloat16 [256, 16, 8192], P('replica', None, 'tensor'), may hold values from -0.0625 to 0.0625
- adapter_up: bfloat16 [256, 16, 6144], P('replica', None, 'tensor'), may hold values from -0.75 to 0.75
- request_adapter: int32 [640], replicated, may hold values from 0 to 255
- key_value_cache: bfloat16 [5120, 16, 2048], P(('replica', 'tensor')), may hold values from -1000 to 1000
- block_table: int32 [640, 8], P(('replica', 'tensor')), may hold values from 0 to 159, as said below
- cache_length: int32 [640], P(('replica', 'tensor')), may hold values from 1 to 128, as said below
- partner: int32 [4, 8], replicated, may hold values from 0 to 3, as said below
- moving: int32 [640], P(('replica', 'tensor')), may hold values from 0 to 1, as said below
Outputs:
- attn_out: bfloat16 [640, 2, 8192], P('replica', None, 'tensor')
- arrived_kv: bfloat16 [64, 128, 2048], P(('replica', 'tensor'))
Inputs may be any that keep to these rules, and one draw needn't show every extreme that they name: `block_table`: the rows of one device (the 20 home slots of one replica and one tensor index) hold every block index of 0 to 159 exactly once. `cache_length`: among the 20 requests of one device one has all 128 positions cached. partner[r, k] = r XOR m_k for one m_k of 1 to 3 for each tensor index k, the same for every replica. Slot s of replica r moves exactly when slot s of replica partner[r, s // 20] does. Each device's 20 slots hold 1 to 2 moving ones, and some device holds 2.
All inputs are finite; a program needn't handle non-finite values.
Results may differ from a plain program's by a relative error of at most 0.035.
Values may be sent and summed in bfloat16 or wider, within the bound.
A program may use at most 256 MiB of HBM per device.

v0:
```python
import jax
import jax.numpy as jnp
from jax import lax
from jax.sharding import PartitionSpec as P

QUERY_HEADS = 32
KEY_VALUE_HEADS = 8
HEAD_SIZE = 128
MIG_DEV = 2


theta_base = 500000.0
norm_eps = 1e-05
adapter_scale = 2.0


def passed_along(array, axis, by):
    length = lax.axis_size(axis)
    return lax.ppermute(array, axis, [(i, (i + by) % length) for i in range(length)])


def rotate(vectors, positions):
    track_count = vectors.shape[-1]
    half_width = track_count // 2
    frequency = jnp.power(
        jnp.float32(theta_base), -jnp.arange(half_width, dtype=jnp.float32) / half_width
    )
    angles = positions.astype(jnp.float32)[..., None] * frequency
    cosine = jnp.cos(angles)
    sine_part = jnp.sin(angles)
    first_half = vectors[..., :half_width].astype(jnp.float32)
    second = vectors[..., half_width:].astype(jnp.float32)
    joined = jnp.concatenate(
        [first_half * cosine - second * sine_part, second * cosine + first_half * sine_part],
        axis=-1,
    )
    return joined.astype(jnp.bfloat16)


def new_entries(projected_rows, lengths):
    item_count = projected_rows.shape[0]
    fresh_tokens = projected_rows.shape[1]
    query_columns = QUERY_HEADS * HEAD_SIZE
    key_columns = KEY_VALUE_HEADS * HEAD_SIZE
    fresh_keys = projected_rows[:, :, query_columns : query_columns + key_columns].reshape(
        item_count, fresh_tokens, KEY_VALUE_HEADS, HEAD_SIZE
    )
    offsets = jnp.arange(fresh_tokens, dtype=jnp.int32)
    positions = lengths[:, None] + offsets[None, :]
    rotated = rotate(fresh_keys, positions[:, :, None]).reshape(
        item_count, fresh_tokens, key_columns
    )
    fresh_values = projected_rows[:, :, query_columns + key_columns :]
    return jnp.concatenate([rotated, fresh_values], axis=-1)


def append_cache(key_value_blocks, entries, lengths, live):
    span = key_value_blocks.shape[1]
    places = jnp.arange(span, dtype=jnp.int32)[None, :]
    kept = jnp.where(
        (places < lengths[:, None])[:, :, None],
        key_value_blocks,
        jnp.zeros((), key_value_blocks.dtype),
    )
    for offset in range(entries.shape[1]):
        written = (places == lengths[:, None] + offset)[:, :, None]
        kept = jnp.where(written, entries[:, offset][:, None, :], kept)
    return jnp.where(live[:, None, None], kept, jnp.zeros((), kept.dtype))


def attend(projected_rows, key_value_blocks, lengths):
    item_count = projected_rows.shape[0]
    fresh_tokens = projected_rows.shape[1]
    head_sharing = QUERY_HEADS // KEY_VALUE_HEADS
    cache_extent = key_value_blocks.shape[1]
    query_columns = QUERY_HEADS * HEAD_SIZE
    key_columns = KEY_VALUE_HEADS * HEAD_SIZE
    query_rows = projected_rows[:, :, :query_columns].reshape(
        item_count, fresh_tokens, KEY_VALUE_HEADS, head_sharing, HEAD_SIZE
    )
    fresh_keys = projected_rows[:, :, query_columns : query_columns + key_columns].reshape(
        item_count, fresh_tokens, KEY_VALUE_HEADS, HEAD_SIZE
    )
    fresh_values = projected_rows[:, :, query_columns + key_columns :].reshape(
        item_count, fresh_tokens, KEY_VALUE_HEADS, HEAD_SIZE
    )
    offsets = jnp.arange(fresh_tokens, dtype=jnp.int32)
    positions = lengths[:, None] + offsets[None, :]
    query_rows = rotate(query_rows, positions[:, :, None, None])
    fresh_keys = rotate(fresh_keys, positions[:, :, None])
    prior_keys = key_value_blocks[:, :, :key_columns].reshape(
        item_count, cache_extent, KEY_VALUE_HEADS, HEAD_SIZE
    )
    prior_values = key_value_blocks[:, :, key_columns:].reshape(
        item_count, cache_extent, KEY_VALUE_HEADS, HEAD_SIZE
    )
    scaling = HEAD_SIZE ** (-0.5)
    old_scores = (
        jnp.einsum("nthgd,nlhd->nthgl", query_rows, prior_keys, preferred_element_type=jnp.float32)
        * scaling
    )
    new_scores = (
        jnp.einsum("nthgd,nshd->nthgs", query_rows, fresh_keys, preferred_element_type=jnp.float32)
        * scaling
    )
    old_valid = jnp.arange(cache_extent, dtype=jnp.int32)[None, :] < lengths[:, None]
    new_valid = offsets[None, :] <= offsets[:, None]
    old_scores = jnp.where(old_valid[:, None, None, None, :], old_scores, -jnp.inf)
    new_scores = jnp.where(new_valid[None, :, None, None, :], new_scores, -jnp.inf)
    highest = jnp.maximum(jnp.max(old_scores, axis=-1), jnp.max(new_scores, axis=-1))
    old_exp = jnp.exp(old_scores - highest[..., None])
    new_exp = jnp.exp(new_scores - highest[..., None])
    totals = jnp.sum(old_exp, axis=-1) + jnp.sum(new_exp, axis=-1)
    old_weights = (old_exp / totals[..., None]).astype(jnp.bfloat16)
    new_weights = (new_exp / totals[..., None]).astype(jnp.bfloat16)
    mixed = jnp.einsum(
        "nthgl,nlhd->nthgd", old_weights, prior_values, preferred_element_type=jnp.float32
    )
    mixed = mixed + jnp.einsum(
        "nthgs,nshd->nthgd", new_weights, fresh_values, preferred_element_type=jnp.float32
    )
    return mixed.reshape(item_count, fresh_tokens, QUERY_HEADS * HEAD_SIZE).astype(jnp.bfloat16)


def per_device(
    hidden_input,
    input_norm_gain,
    merged_weight,
    output_weight,
    adapter_down,
    adapter_up,
    request_adapter,
    key_value_cache,
    block_table,
    cache_length,
    partner,
    moving,
):
    row_local, fresh_tokens, width_local = hidden_input.shape
    tensor_rank = lax.axis_index("tensor")
    replica_rank = lax.axis_index("replica")
    gathered = lax.all_gather(hidden_input, "tensor", axis=2, tiled=True)
    gathered_f = gathered.astype(jnp.float32)
    mean_square = jnp.mean(gathered_f * gathered_f, axis=-1, keepdims=True)
    normed_hidden = (
        gathered_f * lax.rsqrt(mean_square + norm_eps) * input_norm_gain.astype(jnp.float32)
    ).astype(jnp.bfloat16)
    normed_local = lax.dynamic_slice_in_dim(
        normed_hidden, tensor_rank * width_local, width_local, 2
    )
    model_width = normed_hidden.shape[2]
    base_projection = jnp.dot(
        normed_hidden.reshape(-1, model_width), merged_weight, preferred_element_type=jnp.float32
    )
    local_ids = lax.dynamic_slice_in_dim(request_adapter, replica_rank * row_local, row_local, 0)
    all_rows = lax.all_gather(normed_local, "replica", axis=0, tiled=True)
    owned_count = adapter_down.shape[0]
    owned_start = replica_rank * owned_count
    relative = request_adapter - owned_start
    inside = (relative >= 0) & (relative < owned_count)
    chosen = adapter_down[jnp.clip(relative, 0, owned_count - 1)]
    contrib = jnp.einsum("bnd,brd->bnr", all_rows, chosen, preferred_element_type=jnp.float32)
    shrink_part = lax.psum_scatter(
        jnp.where(inside[:, None, None], contrib, 0.0).astype(jnp.bfloat16),
        "replica",
        scatter_dimension=0,
        tiled=True,
    )
    shrink = lax.psum(shrink_part, "tensor").astype(jnp.float32)
    shrink_low = shrink.astype(jnp.bfloat16)
    column_local = adapter_up.shape[2]
    block_tables = lax.all_gather(adapter_up, "replica", axis=0, tiled=True)
    held_count = block_tables.shape[0]
    relative = local_ids
    inside = (relative >= 0) & (relative < held_count)
    chosen = block_tables[jnp.clip(relative, 0, held_count - 1)]
    contrib = jnp.einsum("bnr,brc->bnc", shrink_low, chosen, preferred_element_type=jnp.float32)
    widen_step = jnp.where(inside[:, None, None], contrib, 0.0)
    projected_rows = (
        base_projection.reshape(row_local, fresh_tokens, column_local) + adapter_scale * widen_step
    ).astype(jnp.bfloat16)
    by_request = lax.all_to_all(projected_rows, "tensor", split_axis=0, concat_axis=2, tiled=True)
    slots_local = moving.shape[0]
    track_count = key_value_cache.shape[2]
    moving_slots = jnp.argsort(1 - moving, stable=True)[:MIG_DEV]
    pages_out = block_table[moving_slots]
    outgoing = key_value_cache[pages_out].reshape(MIG_DEV, -1, track_count)
    replicas = lax.axis_size("replica")
    received = jnp.zeros_like(outgoing)
    partner_rank = partner[replica_rank, tensor_rank]
    for distance in range(1, replicas):
        arrived_here = passed_along(outgoing, "replica", distance)
        received = jnp.where(
            partner_rank == (replica_rank - distance) % replicas, arrived_here, received
        )
    slot_blocks = key_value_cache[block_table].reshape(slots_local, -1, track_count)
    arriving = moving[moving_slots] == 1
    current = slot_blocks[moving_slots]
    landed = jnp.where(arriving[:, None, None], received, current)
    slot_blocks = slot_blocks.at[moving_slots].set(landed)
    attended = attend(by_request, slot_blocks, cache_length)
    moved_lengths = cache_length[moving_slots]
    entries = new_entries(by_request[moving_slots], moved_lengths)
    arrived = append_cache(landed, entries, moved_lengths, arriving)
    returned = lax.all_to_all(attended, "tensor", split_axis=2, concat_axis=0, tiled=True)
    heads_local = returned.shape[2]
    partial_value = jnp.dot(
        returned.reshape(-1, heads_local), output_weight, preferred_element_type=jnp.float32
    )
    partial_value = partial_value.reshape(row_local, fresh_tokens, -1)
    summed = lax.psum_scatter(
        partial_value.astype(jnp.bfloat16), "tensor", scatter_dimension=2, tiled=True
    )
    return (summed, arrived)


def solution(mesh):
    placed = (
        P("replica", None, "tensor"),
        P(),
        P(None, "tensor"),
        P("tensor", None),
        P("replica", None, "tensor"),
        P("replica", None, "tensor"),
        P(),
        P(("replica", "tensor"), None, None),
        P(("replica", "tensor"), None),
        P(("replica", "tensor")),
        P(),
        P(("replica", "tensor")),
    )
    return jax.shard_map(
        per_device,
        mesh=mesh,
        in_specs=placed,
        out_specs=(P("replica", None, "tensor"), P(("replica", "tensor"), None, None)),
        check_vma=False,
    )
```

profile of v0, /device:TPU:0, one launch (start us, length us, event | category | flops | bytes accessed | tf_op | source)
XLA Modules:
  0.0 549.4 jit_solution(14254897596119710224)
XLA Ops:
  7.2 0.7 all-gather.4.cloned.1.call-update
  8.0 0.7 all-gather.8.cloned.1.call-update
  8.7 0.7 convert_element_type.86
  9.4 45.2 %all-gather.4.cloned.1.call-done = bf16[160,2,8192]{2,1,0:T(2,128)(2,1)} async-done(((bf16[160,2,1024]{2,1,0:T(2,128)(2,1)}), bf16[160,2,8192]{2,1,0:T(2,128)(2,1)}) %all-gather.4.cloned.1.call-update) | async-done | bytes 5242896 | tf_op jit(solution)/shard_map/all_gather | solution.py:142
  54.7 8.0 %fusion.2 = f32[160,2]{1,0:T(8,128)S(1)} fusion(bf16[160,2,8192]{2,1,0:T(2,128)(2,1)} %all-gather.4.cloned.1.call-done), kind=kLoop, calls=%fused_computation.15 | loop fusion | flops 7864000 | bytes 5244160 | tf_op jit(solution)/shard_map/reduce_sum | solution.py:144
  62.7 7.9 %fusion.4 = bf16[160,2,8192]{2,1,0:T(2,128)(2,1)S(1)} fusion(bf16[160,2,8192]{2,1,0:T(2,128)(2,1)} %all-gather.4.cloned.1.call-done, f32[8192]{0:T(1024)S(1)} %convert_element_type.86, f32[160,2]{1,0:T(8,128)S(1)} %add_rsqrt_fusion), kind=kLoop, calls=%fused_computation.17 | loop fusion | flops 10485760 | bytes 10519808 | tf_op jit(solution)/shard_map/convert_element_type | solution.py:147
  70.7 2.3 copy-done.4
  72.9 1.5 constant_dynamic-slice_fusion.1
  74.6 1.6 sort.17
  76.2 0.6 gather_fusion.2
  76.9 5.6 %gather_fusion.3 = bf16[16,16,2048]{2,1,0:T(8,128)(2,1)} fusion(bf16[160,16,2048]{2,1,0:T(8,128)(2,1)} %param.19, s32[1024]{0:T(1024)S(1)} %pad_clamp_fusion.2), kind=kCustom, calls=%fused_computation.3 | custom fusion | bytes 2097216 | tf_op jit(solution)/shard_map/gather | solution.py:187
  82.5 3.4 collective-permute-start
  85.8 1.3 collective-permute-start.2
  87.1 0.6 gather_fusion.1
  87.8 0.6 gather_fusion.7
  88.4 1.3 dynamic_slice.9
  91.6 0.1 copy.106
  91.8 11.7 %gather_fusion = bf16[160,16,2048]{2,1,0:T(8,128)(2,1)} fusion(bf16[160,16,2048]{2,1,0:T(8,128)(2,1)} %param.19, s32[1024]{0:T(1024)S(1)} %pad_clamp_fusion.4), kind=kCustom, calls=%fused_computation | custom fusion | bytes 20972160 | tf_op jit(solution)/shard_map/gather | solution.py:196
  103.5 4.6 gather_fusion.4
  108.1 15.6 %gather_fusion.5 = bf16[640,16,1024]{2,1,0:T(8,128)(2,1)} fusion(bf16[64,16,1024]{2,1,0:T(8,128)(2,1)S(1)} %copy-done, s32[1024]{0:T(1024)S(1)} %pad_clamp_fusion.1), kind=kCustom, calls=%fused_computation.5 | custom fusion | bytes 41945600 | tf_op jit(solution)/shard_map/gather | solution.py:161
  123.8 0.6 dynamic-slice
  125.4 0.1 multiply_cosine_fusion.1
  125.6 132.9 %all-gather.8.cloned.1.call-done = bf16[256,16,768]{2,1,0:T(8,128)(2,1)} async-done(((bf16[64,16,768]{2,1,0:T(8,128)(2,1)}), bf16[256,16,768]{2,1,0:T(8,128)(2,1)}) %all-gather.8.cloned.1.call-update) | async-done | bytes 6291472 | tf_op jit(solution)/shard_map/all_gather | solution.py:172
  258.5 5.9 %gather_fusion.6 = bf16[160,16,768]{2,1,0:T(8,128)(2,1)} fusion(bf16[256,16,768]{2,1,0:T(8,128)(2,1)} %all-gather.8.cloned.1.call-done, s32[1024]{0:T(1024)S(1)} %pad_clamp_fusion), kind=kCustom, calls=%fused_computation.6 | custom fusion | bytes 7864960 | tf_op jit(solution)/shard_map/gather | solution.py:176
  264.3 50.1 %all-gather.6.cloned.1.call-done = bf16[640,2,1024]{2,1,0:T(2,128)(2,1)} async-done(((bf16[160,2,1024]{2,1,0:T(2,128)(2,1)}), bf16[640,2,1024]{2,1,0:T(2,128)(2,1)}) %all-gather.6.cloned.1.call-update) | async-done | bytes 2621456 | tf_op jit(solution)/shard_map/all_gather | solution.py:156
  314.4 11.9 %fusion.23 = bf16[640,2,16]{2,1,0:T(2,128)(2,1)S(1)} fusion(bf16[640,2,1024]{2,1,0:T(2,128)(2,1)} %all-gather.6.cloned.1.call-done, bf16[640,16,1024]{2,1,0:T(8,128)(2,1)} %gather_fusion.5, pred[640]{0:T(1024)(128)(4,1)S(1)} %compare_and_fusion), kind=kOutput, calls=%fused_computation.34 | convolution fusion | flops 41984000 | bytes 23634560 | tf_op jit(solution)/shard_map/bnd,brd->bnr/dot_general | solution.py:162
  326.3 23.1 %all-reduce = bf16[640,2,16]{2,1,0:T(2,128)(2,1)S(1)} all-reduce(bf16[640,2,16]{2,1,0:T(2,128)(2,1)S(1)} %fusion.23), channel_id=2, replica_groups=mesh['replica'=4,'tensor'=8] {'replica'}, use_global_device_ids=true, to_apply=%region_3.4.clone | all-reduce | flops 20480 | bytes 81920
  349.4 23.6 %psum.7 = bf16[160,2,16]{2,1,0:T(2,128)(2,1)S(1)} all-reduce(bf16[160,2,16]{2,1,0:T(2,128)(2,1)S(1)} %constant_dynamic-slice_fusion), channel_id=1, replica_groups=mesh['replica'=4,'tensor'=8] {'tensor'}, use_global_device_ids=true, to_apply=%region_4.5 | all-reduce | flops 5120 | bytes 20480 | tf_op jit(solution)/shard_map/psum | solution.py:169
  373.1 2.8 fusion.51
  375.8 15.6 %fusion.12 = bf16[160,2,768]{2,0,1:T(8,128)(2,1)S(1)} fusion(bf16[8192,768]{1,0:T(8,128)(2,1)} %param.14, bf16[160,2,8192]{2,1,0:T(2,128)(2,1)} %copy-done.4, f32[160,2,768]{2,1,0:T(2,128)S(1)} %fusion.51, pred[160]{0:T(512)(128)(4,1)S(1)} %compare_and_fusion.1), kind=kOutput, calls=%fused_computation.21 | convolution fusion | flops 4027514880 | bytes 19300512 | tf_op jit(solution)/shard_map/dot_general | solution.py:152
  391.4 1.3 copy.114
  392.7 3.5 all-to-all-start
  396.3 0.4 multiply_cosine_fusion
  396.6 8.9 %all-to-all-done = bf16[160,2,768]{2,1,0:T(2,128)(2,1)S(1)} async-done(((bf16[160,2,768]{2,1,0:T(2,128)(2,1)}), bf16[160,2,768]{2,1,0:T(2,128)(2,1)S(1)}, u32[]{:S(2)}, u32[]{:S(2)}) %all-to-all-start) | async-done | bytes 491552 | tf_op jit(solution)/shard_map/all_to_all | solution.py:182
  405.5 0.3 copy.144
  405.9 0.7 gather_fusion.8
  406.7 0.3 slice.84
  407.1 0.2 reshape.296
  407.5 0.4 fusion.47
  407.9 2.7 select_select_fusion
  410.6 3.0 scatter_fusion
  413.6 10.1 %fusion.46 = (bf16[20,128,1024]{2,1,0:T(8,128)(2,1)}, bf16[20,128,1024]{2,1,0:T(8,128)(2,1)}) fusion(bf16[20,128,2048]{2,1,0:T(8,128)(2,1)} %scatter_fusion), kind=kLoop, calls=%fused_computation.112 | loop fusion | bytes 20971520 | tf_op jit(solution)/shard_map/slice | solution.py:91
  423.7 7.9 %copy.109 = bf16[20,128,1024]{1,2,0:T(8,128)(2,1)} copy(bf16[20,128,1024]{2,1,0:T(8,128)(2,1)} %get-tuple-element.20) | data formatting | bytes 10485760 | tf_op jit(solution)/shard_map/slice | solution.py:91
  431.6 0.1 fusion.36
  431.7 0.1 maximum_bitcast_fusion
  431.8 0.4 fusion.26
  432.3 3.3 fusion.50
  435.6 4.3 fusion.49
  439.8 0.1 max.15
  439.9 0.6 fusion.34
  440.6 1.0 fusion.29
  441.5 7.9 %copy.108 = bf16[20,128,1024]{1,2,0:T(8,128)(2,1)} copy(bf16[20,128,1024]{2,1,0:T(8,128)(2,1)} %get-tuple-element.21) | data formatting | bytes 10485760 | tf_op jit(solution)/shard_map/slice | solution.py:94
  449.4 0.1 add.163
  449.5 5.3 fusion.30
  454.9 0.6 fusion.20
  455.5 1.7 copy.137
  457.2 4.7 reshape.400
  461.9 10.0 %all_to_all.33 = bf16[8,2,10240]{2,1,0:T(2,128)(2,1)S(1)} all-to-all(bf16[8,2,10240]{2,1,0:T(2,128)(2,1)S(1)} %reshape.400), channel_id=1, replica_groups=mesh['replica'=4,'tensor'=8] {'tensor'}, dimensions={0} | all-to-all | bytes 655360 | tf_op jit(solution)/shard_map/all_to_all | solution.py:205
  471.9 5.2 reshape.401
  477.1 1.3 copy.138
  478.4 0.3 copy.124
  478.7 8.2 %convolution_convert_fusion = bf16[160,2,8192]{2,0,1:T(8,128)(2,1)} fusion(bf16[512,8192]{1,0:T(8,128)(2,1)} %param.15, bf16[160,2,512]{2,1,0:T(2,128)(2,1)S(1)} %bitcast.80), kind=kOutput, calls=%fused_computation.14 | convolution fusion | flops 2686976000 | bytes 13959168 | tf_op jit(solution)/shard_map/dot_general | solution.py:207
  486.9 53.2 %reduce-scatter.2.cloned.1.call-done = bf16[160,2,1024]{2,0,1:T(8,128)(2,1)} async-done(((bf16[160,2,8192]{2,0,1:T(8,128)(2,1)}), bf16[160,2,1024]{2,0,1:T(8,128)(2,1)}) %reduce-scatter.2.cloned.1.call-update) | async-done | bytes 655376 | tf_op jit(solution)/shard_map/reduce_scatter | solution.py:211
  540.1 2.6 copy.126
  (61 shorter events, 1.5 us)
Async XLA Ops:
  7.2 100.9 %copy-start = (bf16[64,16,1024]{2,1,0:T(8,128)(2,1)S(1)}, bf16[64,16,1024]{2,1,0:T(8,128)(2,1)}, u32[]{:S(2)}) copy-start(bf16[64,16,1024]{2,1,0:T(8,128)(2,1)} %param.16) | copy-start | bytes 6291460
  7.2 47.5 %all-gather.4.cloned.1.call-start = ((), (), s32[]{:S(2)}) async-start(), calls=%async_computation.3 | async-start | bytes 5898240 | tf_op jit(solution)/shard_map/all_gather | solution.py:142
  7.9 250.5 %all-gather.8.cloned.1.call-start = ((), (), s32[]{:S(2)}) async-start(), calls=%async_computation.5 | async-start | bytes 7864320 | tf_op jit(solution)/shard_map/all_gather | solution.py:172
  8.7 305.7 %all-gather.6.cloned.1.call-start = ((), (), s32[]{:S(2)}) async-start(), calls=%async_computation.4 | async-start | bytes 3276800 | tf_op jit(solution)/shard_map/all_gather | solution.py:156
  62.7 11.8 %copy-start.6 = (s32[20,8]{0,1:T(8,128)S(1)}, s32[20,8]{0,1:T(8,128)}, u32[]{:S(2)}) copy-start(s32[20,8]{0,1:T(8,128)} %param.20) | copy-start | bytes 1924
  62.7 11.9 %copy-start.3 = (s32[20]{0:T(128)S(1)}, s32[20]{0:T(128)}, u32[]{:S(2)}) copy-start(s32[20]{0:T(128)} %param.23) | copy-start | bytes 244
  62.7 25.1 %copy-start.2 = (s32[20]{0:T(128)S(1)}, s32[20]{0:T(128)}, u32[]{:S(2)}) copy-start(s32[20]{0:T(128)} %param.21) | copy-start | bytes 244
  70.7 2.3 copy-start.4
  82.5 325.4 %collective-permute-start = (bf16[2,128,2048]{2,1,0:T(8,128)(2,1)}, bf16[2,128,2048]{2,1,0:T(8,128)(2,1)}, u32[]{:S(2)}, u32[]{:S(2)}) collective-permute-start(bf16[2,128,2048]{2,1,0:T(8,128)(2,1)} %bitcast.3), channel_id=1, source_target_pairs={{0,24},{8,0},{16,8},{24,16},{1,25},{9,1},{17,9},{25,17},{2,26},{10... | collective-permute-start | bytes 3145736 | tf_op jit(solution)/shard_map/ppermute | solution.py:19
  85.8 322.1 %collective-permute-start.1 = (bf16[2,128,2048]{2,1,0:T(8,128)(2,1)}, bf16[2,128,2048]{2,1,0:T(8,128)(2,1)}, u32[]{:S(2)}, u32[]{:S(2)}) collective-permute-start(bf16[2,128,2048]{2,1,0:T(8,128)(2,1)} %bitcast.3), channel_id=1, source_target_pairs={{0,16},{8,24},{16,0},{24,8},{1,17},{9,25},{17,1},{25,9},{2,18},{10... | collective-permute-start | bytes 3145736 | tf_op jit(solution)/shard_map/ppermute | solution.py:19
  85.8 322.1 %collective-permute-start.2 = (bf16[2,128,2048]{2,1,0:T(8,128)(2,1)}, bf16[2,128,2048]{2,1,0:T(8,128)(2,1)}, u32[]{:S(2)}, u32[]{:S(2)}) collective-permute-start(bf16[2,128,2048]{2,1,0:T(8,128)(2,1)} %bitcast.3), channel_id=1, source_target_pairs={{0,8},{8,16},{16,24},{24,0},{1,9},{9,17},{17,25},{25,1},{2,10},{10... | collective-permute-start | bytes 3145736 | tf_op jit(solution)/shard_map/ppermute | solution.py:19
  91.8 16.3 %copy-start.5 = (s32[640]{0:T(1024)S(1)}, s32[640]{0:T(1024)}, u32[]{:S(2)}) copy-start(s32[640]{0:T(1024)} %param.18) | copy-start | bytes 7684
  108.1 15.6 %copy-start.7 = (u32[32]{0:T(128)S(1)}, u32[32]{0:T(128)}, u32[]{:S(2)}) copy-start(u32[32]{0:T(128)} %constant.98) | copy-start | bytes 388
  392.7 12.8 %all-to-all-start = ((bf16[160,2,768]{2,1,0:T(2,128)(2,1)}), bf16[160,2,768]{2,1,0:T(2,128)(2,1)S(1)}, u32[]{:S(2)}, u32[]{:S(2)}) async-start(bf16[160,2,768]{2,1,0:T(2,128)(2,1)} %copy.114), calls=%async_computation | async-start | bytes 983040 | tf_op jit(solution)/shard_map/all_to_all | solution.py:182
  396.2 143.9 %reduce-scatter.2.cloned.1.call-start = ((), (), s32[]{:S(2)}) async-start(), calls=%async_computation.6 | async-start | bytes 5898240 | tf_op jit(solution)/shard_map/reduce_scatter | solution.py:211
  478.7 64.0 %copy-start.1 = (bf16[64,16,1024]{2,1,0:T(8,128)(2,1)S(1)}, bf16[64,16,1024]{2,1,0:T(8,128)(2,1)}, u32[]{:S(2)}) copy-start(bf16[64,16,1024]{2,1,0:T(8,128)(2,1)} %param.16) | copy-start | bytes 6291460
Sparse Core Ops, SparseCore 0:
  9.9 44.7 all-gather.3
  56.2 202.1 all-gather.7
  260.6 53.7 all-gather.5
  487.0 52.9 reduce-scatter.1
where the time goes:
time: 556 us; the launch traced here: 549 us
  waiting for transfers between devices  292 us (53%)
  local copies, waits for them, and re-layouts  99.4 us (18%)
  blocking collectives  56.7 us (10%)
  matrix products  51.9 us (9%)
  other arithmetic  24.6 us (4%)
  between operations  16.9 us (3%)
  starting transfers between devices  8.3 us (1%)
    all_gather x1, waiting for transfers between devices, per_device(): block_tables = lax.all_gather(adapter_up, 'replica', axis=0, tiled=True)  133 us
    reduce_scatter x1, waiting for transfers between devices, per_device(): lax.psum_scatter(partial_value.astype(jnp.bfloat16), 'tensor', scatter_di...  53.2 us
    all_gather x1, waiting for transfers between devices, per_device(): all_rows = lax.all_gather(normed_local, 'replica', axis=0, tiled=True)  50.1 us
    all_gather x1, waiting for transfers between devices, per_device(): gathered = lax.all_gather(hidden_input, 'tensor', axis=2, tiled=True)  45.2 us
    psum x1, blocking collectives, per_device(): shrink = lax.psum(shrink_part, 'tensor').astype(jnp.float32)  23.6 us
    unnamed x1, blocking collectives  23.1 us
    slice x2, local copies, waits for them, and re-layouts, attend(): key_value_blocks[:, :, :key_columns]  18 us
    gather x1, local copies, waits for them, and re-layouts, per_device(): chosen = adapter_down[jnp.clip(relative, 0, owned_count - 1)]  15.6 us
  transfers between devices with their start and end apart: 8, of which 5 were waited for; matrix products, arithmetic and copies ran while one was open for 19% of the time, Pallas kernels for 0%

commit v1 on v0

v1 whole, which is shorter than its diff:
```python
import jax
import jax.numpy as jnp
from jax import lax
from jax.experimental import pallas as pl
from jax.experimental.pallas import tpu as pltpu
from jax.sharding import PartitionSpec as P

QUERY_HEADS = 32
KEY_VALUE_HEADS = 8
HEAD_SIZE = 128
MIG_DEV = 2
FRESH_PAD = 16

theta_base = 500000.0
norm_eps = 1e-05
adapter_scale = 2.0


def rotate(vectors, positions):
    half_width = vectors.shape[-1] // 2
    frequency = jnp.power(
        jnp.float32(theta_base), -jnp.arange(half_width, dtype=jnp.float32) / half_width
    )
    angles = positions.astype(jnp.float32)[..., None] * frequency
    cosine = jnp.cos(angles)
    sine = jnp.sin(angles)
    first = vectors[..., :half_width].astype(jnp.float32)
    second = vectors[..., half_width:].astype(jnp.float32)
    return jnp.concatenate(
        [first * cosine - second * sine, second * cosine + first * sine], axis=-1
    ).astype(jnp.bfloat16)


def pick_blocks(pages, cache):
    count = pages.shape[0]

    def kernel(pages_ref, cache_ref, out_ref, sem):
        def issue(i, carry):
            pltpu.make_async_copy(cache_ref.at[pages_ref[i]], out_ref.at[i], sem).start()
            return carry

        lax.fori_loop(0, count, issue, 0)
        pltpu.make_async_copy(out_ref, out_ref, sem).wait()

    return pl.pallas_call(
        kernel,
        out_shape=jax.ShapeDtypeStruct((count,) + cache.shape[1:], cache.dtype),
        in_specs=[
            pl.BlockSpec(memory_space=pltpu.SMEM),
            pl.BlockSpec(memory_space=pl.ANY),
        ],
        out_specs=pl.BlockSpec(memory_space=pl.ANY),
        scratch_shapes=[pltpu.SemaphoreType.DMA],
    )(pages, cache)


def attend(tables, lengths, moving, spots, cache, landed, queries, fresh, fresh_tokens):
    slots = lengths.shape[0]
    blocks = tables.shape[0] // slots
    block_rows, tracks = cache.shape[1:]
    span = blocks * block_rows
    sharing = QUERY_HEADS // KEY_VALUE_HEADS
    group = fresh_tokens * sharing
    query_rows = KEY_VALUE_HEADS * group
    keys = KEY_VALUE_HEADS * HEAD_SIZE
    total = span + FRESH_PAD

    def kernel(tab, lens, mov, spot, cache_ref, landed_ref, q_ref, fresh_ref, out_ref, kv, sems):
        def issue(s, carry):
            @pl.when(mov[s] == 0)
            def _():
                for b in range(blocks):
                    pltpu.make_async_copy(
                        cache_ref.at[tab[s * blocks + b]],
                        kv.at[s, pl.ds(b * block_rows, block_rows)],
                        sems.at[s],
                    ).start()

            @pl.when(mov[s] != 0)
            def _():
                pltpu.make_async_copy(
                    landed_ref.at[spot[s]], kv.at[s, pl.ds(0, span)], sems.at[s]
                ).start()

            return carry

        lax.fori_loop(0, slots, issue, 0)

        def work(s, carry):
            kv[s, pl.ds(span, FRESH_PAD), :] = fresh_ref[s]
            whole = kv.at[s, pl.ds(0, span)]
            pltpu.make_async_copy(whole, whole, sems.at[s]).wait()
            scores = []
            for h in range(KEY_VALUE_HEADS):
                q = q_ref[s, h * group : (h + 1) * group, :].astype(jnp.bfloat16)
                k = kv[s, :, h * HEAD_SIZE : (h + 1) * HEAD_SIZE]
                scores.append(
                    lax.dot_general(
                        q, k, (((1,), (1,)), ((), ())), preferred_element_type=jnp.float32
                    )
                )
            scores = jnp.concatenate(scores, axis=0) * (HEAD_SIZE ** (-0.5))
            row = lax.broadcasted_iota(jnp.int32, (query_rows, total), 0)
            col = lax.broadcasted_iota(jnp.int32, (query_rows, total), 1)
            token = lax.rem(row, group) // sharing
            valid = (col < jnp.minimum(lens[s], span)) | (
                (col >= span) & (col - span <= token)
            )
            scores = jnp.where(valid, scores, -jnp.inf)
            high = jnp.max(scores, axis=-1, keepdims=True)
            raised = jnp.exp(scores - high)
            weights = raised / jnp.sum(raised, axis=-1, keepdims=True)
            mixed = []
            for h in range(KEY_VALUE_HEADS):
                w = weights[h * group : (h + 1) * group].astype(jnp.bfloat16)
                v = kv[s, :, keys + h * HEAD_SIZE : keys + (h + 1) * HEAD_SIZE]
                mixed.append(jnp.dot(w, v, preferred_element_type=jnp.float32))
            out_ref[s] = jnp.concatenate(mixed, axis=0).astype(jnp.bfloat16)
            return carry

        lax.fori_loop(0, slots, work, 0)

    smem = pl.BlockSpec(memory_space=pltpu.SMEM)
    vmem = pl.BlockSpec(memory_space=pltpu.VMEM)
    hbm = pl.BlockSpec(memory_space=pl.ANY)
    return pl.pallas_call(
        kernel,
        out_shape=jax.ShapeDtypeStruct((slots, query_rows, HEAD_SIZE), jnp.bfloat16),
        in_specs=[smem, smem, smem, smem, hbm, hbm, vmem, vmem],
        out_specs=vmem,
        scratch_shapes=[
            pltpu.VMEM((slots, total, tracks), jnp.bfloat16),
            pltpu.SemaphoreType.DMA((slots,)),
        ],
        compiler_params=pltpu.CompilerParams(vmem_limit_bytes=40 * 1024 * 1024),
    )(tables, lengths, moving, spots, cache, landed, queries, fresh)


def per_device(
    hidden_input,
    input_norm_gain,
    merged_weight,
    output_weight,
    adapter_down,
    adapter_up,
    request_adapter,
    key_value_cache,
    block_table,
    cache_length,
    partner,
    moving,
):
    row_local, fresh_tokens, width_local = hidden_input.shape
    tensor_rank = lax.axis_index("tensor")
    replica_rank = lax.axis_index("replica")
    tensors = lax.axis_size("tensor")
    replicas = lax.axis_size("replica")
    rows = row_local * fresh_tokens
    slots = moving.shape[0]
    blocks = block_table.shape[1]
    tracks = key_value_cache.shape[2]
    span = blocks * key_value_cache.shape[1]
    column_local = merged_weight.shape[1]
    owned, rank = adapter_down.shape[:2]
    f32, bf16 = jnp.float32, jnp.bfloat16

    hidden = hidden_input.reshape(rows, width_local)
    all_rows = lax.all_gather(hidden, "replica", axis=0, tiled=True)
    gathered = lax.all_gather(hidden, "tensor", axis=1, tiled=True)

    slot_ids = jnp.arange(slots, dtype=jnp.int32)
    is_moving = moving == 1
    until = slot_ids[None, :] <= slot_ids[:, None]
    order = jnp.sum(jnp.where(until, moving[None, :], 0), axis=1) - 1
    hot = is_moving[None, :] & (order[None, :] == jnp.arange(MIG_DEV)[:, None])
    arriving = jnp.any(hot, axis=1)
    pages_out = jnp.sum(jnp.where(hot[:, :, None], block_table[None], 0), axis=1).reshape(-1)
    received = pick_blocks(pages_out, key_value_cache).reshape(MIG_DEV, span, tracks)
    flips = lax.dynamic_slice(partner, (replica_rank, tensor_rank), (1, 1))[0, 0] ^ replica_rank
    bit = 1
    while bit < replicas:
        pairs = [(i, i ^ bit) for i in range(replicas)]
        other = lax.ppermute(received, "replica", pairs)
        received = jnp.where((flips & bit) != 0, other, received)
        bit *= 2

    local_gain = lax.dynamic_slice_in_dim(
        input_norm_gain, tensor_rank * width_local, width_local, 0
    ).astype(f32)
    scaled_rows = (all_rows.astype(f32) * local_gain).astype(bf16)
    inner = jnp.einsum(
        "nd,cd->nc",
        scaled_rows,
        adapter_down.reshape(owned * rank, width_local),
        preferred_element_type=f32,
    )
    relative = jnp.repeat(request_adapter - replica_rank * owned, fresh_tokens)
    lanes = jnp.arange(owned * rank, dtype=jnp.int32)
    chosen = relative[:, None] == (lanes // rank)[None, :]
    spread = (lanes[None, :] % rank == jnp.arange(rank)[:, None]).astype(bf16)
    part = jnp.einsum(
        "rc,nc->rn", spread, jnp.where(chosen, inner, 0.0).astype(bf16), preferred_element_type=f32
    ).astype(bf16)
    parts = lax.all_gather(part, "tensor", axis=0)
    shrink_low = jnp.sum(parts.astype(f32), axis=0).astype(bf16)
    wide = jnp.einsum("rn,rc->nc", shrink_low, spread, preferred_element_type=f32)
    wide = jnp.where(chosen, wide, 0.0).astype(bf16)
    expand = jnp.dot(
        wide, adapter_up.reshape(owned * rank, column_local), preferred_element_type=f32
    ).astype(bf16)
    expand = lax.psum_scatter(expand, "replica", scatter_dimension=0, tiled=True)

    gathered_f = gathered.astype(f32)
    factor = lax.rsqrt(jnp.mean(gathered_f * gathered_f, axis=-1, keepdims=True) + norm_eps)
    scaled = (gathered_f * input_norm_gain.astype(f32)).astype(bf16)
    base = jnp.dot(scaled, merged_weight, preferred_element_type=f32)
    projected = (factor * (base + adapter_scale * expand.astype(f32))).astype(bf16)

    swapped = lax.all_to_all(
        projected.reshape(tensors, slots * fresh_tokens, column_local),
        "tensor",
        split_axis=0,
        concat_axis=0,
        tiled=True,
    )
    by_request = jnp.transpose(swapped, (1, 0, 2)).reshape(slots, fresh_tokens, -1, HEAD_SIZE)
    key_end = QUERY_HEADS + KEY_VALUE_HEADS
    positions = cache_length[:, None] + jnp.arange(fresh_tokens, dtype=jnp.int32)[None, :]
    rotated = rotate(by_request[:, :, :key_end], positions[:, :, None])
    sharing = QUERY_HEADS // KEY_VALUE_HEADS
    queries = rotated[:, :, :QUERY_HEADS].reshape(
        slots, fresh_tokens, KEY_VALUE_HEADS, sharing, HEAD_SIZE
    )
    queries = jnp.transpose(queries, (0, 2, 1, 3, 4)).reshape(slots, -1, HEAD_SIZE).astype(f32)
    entries = jnp.concatenate(
        [rotated[:, :, QUERY_HEADS:], by_request[:, :, key_end:]], axis=2
    ).reshape(slots, fresh_tokens, tracks)
    fresh = jnp.pad(entries, ((0, 0), (0, FRESH_PAD - fresh_tokens), (0, 0)))
    attended = attend(
        block_table.reshape(-1),
        cache_length,
        moving,
        jnp.clip(order, 0, MIG_DEV - 1),
        key_value_cache,
        received,
        queries,
        fresh,
        fresh_tokens,
    )
    attended = attended.reshape(slots, KEY_VALUE_HEADS, fresh_tokens, sharing * HEAD_SIZE)
    heads_local = output_weight.shape[0]
    attended = jnp.transpose(attended, (0, 2, 1, 3)).reshape(
        slots * fresh_tokens, tensors, heads_local
    )
    returned = lax.all_to_all(
        jnp.transpose(attended, (1, 0, 2)), "tensor", split_axis=0, concat_axis=0, tiled=True
    ).reshape(rows, heads_local)
    partial = jnp.dot(returned, output_weight, preferred_element_type=f32).astype(bf16)
    summed = lax.psum_scatter(partial, "tensor", scatter_dimension=1, tiled=True)

    hot_f = hot.astype(bf16)
    moved = jnp.einsum(
        "js,sc->jc", hot_f, entries.reshape(slots, -1), preferred_element_type=f32
    ).astype(bf16).reshape(MIG_DEV, fresh_tokens, tracks)
    lens = jnp.sum(jnp.where(hot, cache_length[None, :], 0), axis=1)
    places = jnp.arange(span, dtype=jnp.int32)[None, :]
    kept = jnp.where((places < lens[:, None])[:, :, None], received, jnp.zeros((), bf16))
    for offset in range(fresh_tokens):
        written = (places == lens[:, None] + offset)[:, :, None]
        kept = jnp.where(written, moved[:, offset][:, None, :], kept)
    arrived = jnp.where(arriving[:, None, None], kept, jnp.zeros((), bf16))
    return summed.reshape(row_local, fresh_tokens, -1), arrived


def solution(mesh):
    placed = (
        P("replica", None, "tensor"),
        P(),
        P(None, "tensor"),
        P("tensor", None),
        P("replica", None, "tensor"),
        P("replica", None, "tensor"),
        P(),
        P(("replica", "tensor"), None, None),
        P(("replica", "tensor"), None),
        P(("replica", "tensor")),
        P(),
        P(("replica", "tensor")),
    )
    return jax.shard_map(
        per_device,
        mesh=mesh,
        in_specs=placed,
        out_specs=(P("replica", None, "tensor"), P(("replica", "tensor"), None, None)),
        check_vma=False,
    )
```

time: 556 us -> 358 us (0.64); the launches traced: 549 us -> 358 us
  waiting for transfers between devices: 292 us -> 200 us
  local copies, waits for them, and re-layouts: 99.4 us -> 14.2 us
  Pallas kernels: 0 us -> 59.5 us
  blocking collectives: 56.7 us -> 22.6 us
  matrix products: 51.9 us -> 30.6 us
  other arithmetic: 24.6 us -> 10.6 us
    all_gather x3 -> x2, waiting for transfers between devices: 228 us -> 55.1 us  [the longest x1 55.1 us: per_device(): all_rows = lax.all_gather(hidden, 'replica', axis=0, tiled=True)]
    pallas_call x0 -> x2, Pallas kernels: none -> 59.5 us  [the longest x1 33.7 us: pick_blocks(): pl.pallas_call(kernel, out_shape=jax.ShapeDtypeStruct((count,) + cache.sh...]
    reduce_scatter x1 -> x2, waiting for transfers between devices: 53.2 us -> 100 us  [the longest x1 55.2 us: per_device(): lax.psum_scatter(partial, 'tensor', scatter_dimension=1, tiled=True)]
    gather x9 -> x0, local copies, waits for them, and re-layouts: 45.8 us -> none  [the longest x1 15.6 us: per_device(): chosen = adapter_down[jnp.clip(relative, 0, owned_count - 1)]]
    ppermute x3 -> x2, waiting for transfers between devices: 0.01 us -> 37.9 us  [per_device(): other = lax.ppermute(received, 'replica', pairs)]
    slice x7 -> x1, local copies, waits for them, and re-layouts: 26.7 us -> 0.02 us  [per_device(): by_request[:, :, key_end:]]
    psum x1 -> x0, blocking collectives: 23.6 us -> none  [per_device(): shrink = lax.psum(shrink_part, 'tensor').astype(jnp.float32)]
    unnamed x1 -> x0, blocking collectives: 23.1 us -> none
  transfers between devices with their start and end apart: 8 -> 7, of which waited for: 5 -> 5; matrix products, arithmetic and copies ran while one was open for 19% -> 10% of each run, Pallas kernels for 0% -> 9%
where the time goes in v1:
time: 358 us
  waiting for transfers between devices  200 us (56%)
  Pallas kernels  59.5 us (17%)
  matrix products  30.6 us (9%)
  blocking collectives  22.6 us (6%)
  between operations  14.7 us (4%)
  local copies, waits for them, and re-layouts  14.2 us (4%)
  other arithmetic  10.6 us (3%)
  starting transfers between devices  5.6 us (2%)
    reduce_scatter x1, waiting for transfers between devices, per_device(): lax.psum_scatter(partial, 'tensor', scatter_dimension=1, tiled=True)  55.2 us
    all_gather x1, waiting for transfers between devices, per_device(): all_rows = lax.all_gather(hidden, 'replica', axis=0, tiled=True)  55.1 us
    reduce_scatter x1, waiting for transfers between devices, per_device(): lax.psum_scatter(expand, 'replica', scatter_dimension=0, tiled=True)  45.3 us
    ppermute x2, waiting for transfers between devices, per_device(): other = lax.ppermute(received, 'replica', pairs)  37.9 us
    pallas_call x1, Pallas kernels, pick_blocks(): pl.pallas_call(kernel, out_shape=jax.ShapeDtypeStruct((count,) + cache.sh...  33.7 us
    pallas_call x1, Pallas kernels, attend(): pl.pallas_call(kernel, out_shape=jax.ShapeDtypeStruct((slots, query_rows,...  25.9 us
    all_to_all x1, blocking collectives, per_device(): lax.all_to_all(jnp.transpose(attended, (1, 0, 2)), 'tensor', split_axis=0...  11.8 us
    dot_general x1, matrix products, per_device(): base = jnp.dot(scaled, merged_weight, preferred_element_type=f32)  11.1 us
  transfers between devices with their start and end apart: 7, of which 5 were waited for; matrix products, arithmetic and copies ran while one was open for 10% of the time, Pallas kernels for 9%

profile of v1, /device:TPU:0, one launch (start us, length us, event | category | flops | bytes accessed | tf_op | source)
XLA Modules:
  0.0 357.5 jit_solution(6926318260606868767)
XLA Ops:
  7.2 0.0 copy-start
  7.2 0.0 all-gather.6.cloned.1.call-start
  7.2 2.9 reshape.240
  10.1 0.0 all-gather.6.cloned.1.call-update
  10.1 0.0 all-gather.4.cloned.1.call-start
  10.2 0.7 all-gather.4.cloned.1.call-update
  10.9 0.0 reduce-scatter.3.cloned.1.call-start
  10.9 0.7 broadcast_subtract_fusion
  11.6 0.2 broadcast_in_dim.137
  11.8 0.2 eq.96
  12.0 0.7 dynamic-slice_convert_fusion
  12.7 55.1 %all-gather.6.cloned.1.call-done = bf16[1280,1024]{1,0:T(8,128)(2,1)} async-done(((bf16[320,1024]{1,0:T(8,128)(2,1)}), bf16[1280,1024]{1,0:T(8,128)(2,1)}) %all-gather.6.cloned.1.call-update) | async-done | bytes 2621456 | tf_op jit(solution)/shard_map/all_gather | solution.py:168
  67.8 0.0 copy-done
  67.8 5.3 %convolution_convert_fusion.3 = bf16[16,1280]{1,0:T(8,128)(2,1)S(1)} fusion(bf16[1024,1024]{1,0:T(8,128)(2,1)S(1)} %bitcast.41, bf16[1280,1024]{1,0:T(8,128)(2,1)} %all-gather.6.cloned.1.call-done, f32[1024]{0:T(1024)S(1)} %dynamic-slice_convert_fusion, s32[1024]{0:T(1024)S(1)} %get-tuple-element.17, s32[1280]{0:T(1024)S(1)} %eq.96, ...), kind=kOutput, calls=%fused_computation.15 | convolution fusion | flops 2734198784 | bytes 4776960 | tf_op jit(solution)/shard_map/rc,nc->rn/dot_general | solution.py:201
  73.1 10.8 %all-gather = bf16[128,1280]{1,0:T(8,128)(2,1)S(1)} all-gather(bf16[16,1280]{1,0:T(8,128)(2,1)S(1)} %convolution_convert_fusion.3), channel_id=2, replica_groups=mesh['replica'=4,'tensor'=8] {'tensor'}, dimensions={0}, use_global_device_ids=true | all-gather | bytes 368640 | tf_op jit(solution)/shard_map/all_gather | solution.py:204
  83.9 0.0 copy-start.4
  84.0 0.0 copy-start.3
  84.0 0.0 copy-start.8
  84.0 5.8 %convolution_convert_fusion.2 = bf16[1280,768]{1,0:T(8,128)(2,1)} fusion(bf16[1024,768]{1,0:T(8,128)(2,1)} %bitcast.54, bf16[16,1280]{1,0:T(8,128)(2,1)S(1)} %reduce_sum.51, s32[1024]{0:T(1024)S(1)} %get-tuple-element.17, s32[1280]{0:T(1024)S(1)} %eq.96, s32[1024]{0:T(1024)S(1)} %get-tuple-element.16), kind=kOutput, calls=%fused_computation.13 | convolution fusion | flops 2060140544 | bytes 3593216 | tf_op jit(solution)/shard_map/dot_general | solution.py:208
  89.8 0.0 reduce-scatter.3.cloned.1.call-update
  89.8 0.1 select_reduce_fusion
  90.0 0.1 select_reduce_fusion.2
  90.1 0.2 select_reduce_fusion.1
  90.2 0.6 reshape.238.pages_ref
  90.9 33.7 %shard_map.131 = bf16[16,16,2048]{2,1,0:T(8,128)(2,1)} custom-call(s32[16]{0:T(128)} %reshape.238.pages_ref, bf16[160,16,2048]{2,1,0:T(8,128)(2,1)} %cache_ref.3), custom_call_target="tpu_custom_call" | custom-call | tf_op jit(solution)/shard_map/pallas_call | solution.py:45
  124.6 0.1 collective-permute-start
  124.7 0.1 copy.35
  124.8 1.3 dynamic_slice.6
  126.7 0.1 reduce_or.9
  126.8 0.1 reshape.237.tab
  126.9 0.1 iota_compare_fusion.6
  127.0 0.1 add_convert_fusion
  127.1 0.4 multiply_cosine_fusion
  127.5 0.0 all-gather.4.cloned.1.call-done
  127.5 3.6 %fusion = f32[320]{0:T(512)S(1)} fusion(bf16[320,8192]{1,0:T(8,128)(2,1)} %all-gather.4.cloned.1.call-done), kind=kLoop, calls=%fused_computation.3 | loop fusion | flops 7864000 | bytes 5244160 | tf_op jit(solution)/shard_map/reduce_sum | solution.py:214
  131.2 45.3 %reduce-scatter.3.cloned.1.call-done = bf16[320,768]{1,0:T(8,128)(2,1)} async-done(((bf16[1280,768]{1,0:T(8,128)(2,1)}), bf16[320,768]{1,0:T(8,128)(2,1)}) %reduce-scatter.3.cloned.1.call-update) | async-done | bytes 491536 | tf_op jit(solution)/shard_map/reduce_scatter | solution.py:211
  176.5 11.1 %fusion.14 = bf16[320,768]{1,0:T(8,128)(2,1)} fusion(bf16[8192,768]{1,0:T(8,128)(2,1)} %param.14, bf16[320,8192]{1,0:T(8,128)(2,1)} %all-gather.4.cloned.1.call-done, f32[8192]{0:T(1024)S(1)} %convert_element_type.74, bf16[320,768]{1,0:T(8,128)(2,1)} %reduce-scatter.3.cloned.1.call-done, f32[320]{0:T(512)S(1)} %add_rsqrt_fusion), kind=kOutput, calls=%fused_computation.18 | convolution fusion | flops 4035624960 | bytes 18842880 | tf_op jit(solution)/shard_map/dot_general | solution.py:216
  187.6 3.7 %all-to-all-start = ((bf16[8,40,768]{2,1,0:T(8,128)(2,1)}), bf16[8,40,768]{2,1,0:T(8,128)(2,1)S(1)}, u32[]{:S(2)}, u32[]{:S(2)}) async-start(bf16[8,40,768]{2,1,0:T(8,128)(2,1)} %bitcast.5), calls=%async_computation.1 | async-start | bytes 983040 | tf_op jit(solution)/shard_map/all_to_all | solution.py:219
  191.2 0.0 reduce-scatter.5.cloned.1.call-start
  191.3 0.0 collective-permute-done
  191.3 1.0 copy-done.6
  192.3 1.3 broadcast_select_fusion
  193.6 1.7 collective-permute-start.1
  195.3 5.3 %all-to-all-done = bf16[8,40,768]{2,1,0:T(8,128)(2,1)S(1)} async-done(((bf16[8,40,768]{2,1,0:T(8,128)(2,1)}), bf16[8,40,768]{2,1,0:T(8,128)(2,1)S(1)}, u32[]{:S(2)}, u32[]{:S(2)}) %all-to-all-start) | async-done | bytes 491552 | tf_op jit(solution)/shard_map/all_to_all | solution.py:219
  200.6 0.1 copy.36
  200.7 0.4 reshape.244
  201.1 0.4 fusion.18
  201.5 0.1 fusion.23
  201.7 0.1 copy.42
  201.8 0.2 pad.4.fresh_ref
  202.0 0.2 fusion.22
  202.2 0.1 copy.37
  202.3 0.2 convolution_convert_fusion.1
  202.5 37.9 %collective-permute-done.1 = bf16[2,128,2048]{2,1,0:T(8,128)(2,1)} collective-permute-done((bf16[2,128,2048]{2,1,0:T(8,128)(2,1)S(1)}, bf16[2,128,2048]{2,1,0:T(8,128)(2,1)}, u32[]{:S(2)}, u32[]{:S(2)}) %collective-permute-start.1) | collective-permute-done | bytes 1048608 | tf_op jit(solution)/shard_map/ppermute | solution.py:183
  240.4 2.5 select_select_fusion
  242.9 4.0 %copy-done.2 = bf16[160,16,2048]{2,1,0:T(8,128)(2,1)S(1)} copy-done((bf16[160,16,2048]{2,1,0:T(8,128)(2,1)S(1)}, bf16[160,16,2048]{2,1,0:T(8,128)(2,1)}, u32[]{:S(2)}) %copy-start.2) | copy-done | bytes 10485784
  246.9 25.9 %shard_map.132 = bf16[20,64,128]{2,1,0:T(8,128)(2,1)S(1)} custom-call(s32[160]{0:T(256)S(1)} %reshape.237.tab, s32[20]{0:T(128)S(1)} %copy-done.3, s32[20]{0:T(128)S(1)} %copy-done.4, s32[20]{0:T(128)S(1)} %get-tuple-element.15.spot, bf16[160,16,2048]{2,1,0:T(8,128)(2,1)S(1)} %copy-done.2, bf16[2,128,2048]{2,1,0:T(8,128)(2,1)S(1)} %get-tuple-element.3.landed_ref, ...), custom_call_target="tpu_custom_call" | custom-call | tf_op jit(solution)/shard_map/pallas_call | solution.py:126
  272.8 0.1 reshape.246
  273.0 0.1 copy.39
  273.1 11.8 %all_to_all.10 = bf16[8,40,512]{2,1,0:T(8,128)(2,1)S(1)} all-to-all(bf16[8,40,512]{2,1,0:T(8,128)(2,1)S(1)} %copy.39), channel_id=1, replica_groups=mesh['replica'=4,'tensor'=8] {'tensor'}, dimensions={0} | all-to-all | bytes 655360 | tf_op jit(solution)/shard_map/all_to_all | solution.py:255
  284.9 8.3 %convolution_convert_fusion = bf16[320,8192]{1,0:T(8,128)(2,1)} fusion(bf16[320,512]{1,0:T(8,128)(2,1)S(1)} %bitcast.52, bf16[512,8192]{1,0:T(8,128)(2,1)} %param.15), kind=kOutput, calls=%fused_computation.2 | convolution fusion | flops 2686976000 | bytes 13959168 | tf_op jit(solution)/shard_map/dot_general | solution.py:258
  293.1 0.0 reduce-scatter.5.cloned.1.call-update
  293.2 55.2 %reduce-scatter.5.cloned.1.call-done = bf16[320,1024]{1,0:T(8,128)(2,1)} async-done(((bf16[320,8192]{1,0:T(8,128)(2,1)}), bf16[320,1024]{1,0:T(8,128)(2,1)}) %reduce-scatter.5.cloned.1.call-update) | async-done | bytes 655376 | tf_op jit(solution)/shard_map/reduce_scatter | solution.py:259
  348.3 2.6 reshape.249
  (24 shorter events, 0.2 us)
Async XLA Ops:
  7.2 60.6 %copy-start = (bf16[64,16,1024]{2,1,0:T(8,128)(2,1)S(1)}, bf16[64,16,1024]{2,1,0:T(8,128)(2,1)}, u32[]{:S(2)}) copy-start(bf16[64,16,1024]{2,1,0:T(8,128)(2,1)} %param.16) | copy-start | bytes 6291460
  7.2 60.6 %all-gather.6.cloned.1.call-start = ((), (), s32[]{:S(2)}) async-start(), calls=%async_computation.5 | async-start | bytes 3276800 | tf_op jit(solution)/shard_map/all_gather | solution.py:168
  10.1 117.4 %all-gather.4.cloned.1.call-start = ((), (), s32[]{:S(2)}) async-start(), calls=%async_computation.4 | async-start | bytes 5898240 | tf_op jit(solution)/shard_map/all_gather | solution.py:169
  10.9 165.6 %reduce-scatter.3.cloned.1.call-start = ((), (), s32[]{:S(2)}) async-start(), calls=%async_computation.6 | async-start | bytes 2457600 | tf_op jit(solution)/shard_map/reduce_scatter | solution.py:211
  83.9 5.9 %copy-start.4 = (s32[20]{0:T(128)S(1)}, s32[20]{0:T(128)}, u32[]{:S(2)}) copy-start(s32[20]{0:T(128)} %mov.1) | copy-start | bytes 244
  84.0 6.0 %copy-start.3 = (s32[20]{0:T(128)S(1)}, s32[20]{0:T(128)}, u32[]{:S(2)}) copy-start(s32[20]{0:T(128)} %lens.1) | copy-start | bytes 244
  84.0 6.1 %copy-start.8 = (s32[20,8]{0,1:T(8,128)S(1)}, s32[20,8]{0,1:T(8,128)}, u32[]{:S(2)}) copy-start(s32[20,8]{0,1:T(8,128)} %param.20) | copy-start | bytes 1924
  90.9 33.8 %copy-start.7 = (bf16[8192]{0:T(1024)(128)(2,1)S(1)}, bf16[8192]{0:T(1024)(128)(2,1)}, u32[]{:S(2)}) copy-start(bf16[8192]{0:T(1024)(128)(2,1)} %param.13) | copy-start | bytes 49156
  124.6 66.7 %collective-permute-start = (bf16[2,128,2048]{2,1,0:T(8,128)(2,1)}, bf16[2,128,2048]{2,1,0:T(8,128)(2,1)S(1)}, u32[]{:S(2)}, u32[]{:S(2)}) collective-permute-start(bf16[2,128,2048]{2,1,0:T(8,128)(2,1)} %bitcast.43), channel_id=1, source_target_pairs={{0,8},{8,0},{16,24},{24,16},{1,9},{9,1},{17,25},{25,17},{2,10},{10... | collective-permute-start | bytes 3145736 | tf_op jit(solution)/shard_map/ppermute | solution.py:183
  131.2 61.1 %copy-start.5 = (bf16[16,16,2048]{2,1,0:T(8,128)(2,1)S(1)}, bf16[16,16,2048]{2,1,0:T(8,128)(2,1)}, u32[]{:S(2)}) copy-start(bf16[16,16,2048]{2,1,0:T(8,128)(2,1)} %shard_map.131) | copy-start | bytes 3145732
  187.6 13.1 %all-to-all-start = ((bf16[8,40,768]{2,1,0:T(8,128)(2,1)}), bf16[8,40,768]{2,1,0:T(8,128)(2,1)S(1)}, u32[]{:S(2)}, u32[]{:S(2)}) async-start(bf16[8,40,768]{2,1,0:T(8,128)(2,1)} %bitcast.5), calls=%async_computation.1 | async-start | bytes 983040 | tf_op jit(solution)/shard_map/all_to_all | solution.py:219
  191.2 157.1 %reduce-scatter.5.cloned.1.call-start = ((), (), s32[]{:S(2)}) async-start(), calls=%async_computation.7 | async-start | bytes 5898240 | tf_op jit(solution)/shard_map/reduce_scatter | solution.py:259
  191.3 1.0 copy-start.6
  193.6 46.8 %collective-permute-start.1 = (bf16[2,128,2048]{2,1,0:T(8,128)(2,1)S(1)}, bf16[2,128,2048]{2,1,0:T(8,128)(2,1)}, u32[]{:S(2)}, u32[]{:S(2)}) collective-permute-start(bf16[2,128,2048]{2,1,0:T(8,128)(2,1)S(1)} %broadcast_select_fusion), channel_id=1, source_target_pairs={{0,16},{8,24},{16,0},{24,8},{1,17},{9,25},{17,1},{25,9},{2,18},{10... | collective-permute-start | bytes 3145736 | tf_op jit(solution)/shard_map/ppermute | solution.py:183
  242.9 4.0 %copy-start.2 = (bf16[160,16,2048]{2,1,0:T(8,128)(2,1)S(1)}, bf16[160,16,2048]{2,1,0:T(8,128)(2,1)}, u32[]{:S(2)}) copy-start(bf16[160,16,2048]{2,1,0:T(8,128)(2,1)} %cache_ref.3) | copy-start | bytes 31457284
  284.9 66.1 %copy-start.1 = (bf16[64,16,1024]{2,1,0:T(8,128)(2,1)S(1)}, bf16[64,16,1024]{2,1,0:T(8,128)(2,1)}, u32[]{:S(2)}) copy-start(bf16[64,16,1024]{2,1,0:T(8,128)(2,1)} %param.16) | copy-start | bytes 6291460
Sparse Core Ops, SparseCore 0:
  10.2 57.4 all-gather.5
  70.2 39.9 all-gather.3
  112.5 63.8 reduce-scatter.2
  293.3 55.0 reduce-scatter.4

commit v2 on v1

--- a/solution.py
+++ b/solution.py
@@ -49,9 +49,122 @@
             pl.BlockSpec(memory_space=pltpu.SMEM),
             pl.BlockSpec(memory_space=pl.ANY),
         ],
-        out_specs=pl.BlockSpec(memory_space=pl.ANY),
+        out_specs=pl.BlockSpec(memory_space=pltpu.VMEM),
         scratch_shapes=[pltpu.SemaphoreType.DMA],
+        compiler_params=pltpu.CompilerParams(vmem_limit_bytes=16 * 1024 * 1024),
     )(pages, cache)
+
+
+def project_out(values, weight, tensors):
+    rows, depth = values.shape
+    width = weight.shape[1] // tensors
+    chips = tensors // 2
+    tile = 256
+    turns = list(range(1, chips)) + [0]
+    bf16, f32 = jnp.bfloat16, jnp.float32
+
+    def kernel(a_ref, w_ref, out_ref, theirs, got, merged, landed, acc, ps, pr, cs, cr):
+        me = lax.axis_index("tensor")
+        core = lax.rem(me, 2)
+        chip = me // 2
+        sibling = me + 1 - 2 * core
+        others = [lax.rem(chip + d, chips) * 2 + core for d in range(1, chips)]
+        barrier = pltpu.get_barrier_semaphore()
+        for peer in [sibling] + others:
+            pl.semaphore_signal(
+                barrier,
+                inc=1,
+                device_id={"tensor": peer},
+                device_id_type=pl.DeviceIdType.MESH,
+            )
+        pl.semaphore_wait(barrier, chips)
+
+        def columns(owner, j):
+            return pl.ds(pl.multiple_of(owner * width + j * tile, tile), tile)
+
+        def here(j):
+            return pl.ds(pl.multiple_of(j * tile, tile), tile)
+
+        first, second = [], []
+        for i, d in enumerate(turns):
+            owner = lax.rem(chip + d, chips) * 2 + 1 - core
+
+            @pl.loop(0, width // tile)
+            def _(j, i=i, owner=owner):
+                theirs[i, :, here(j)] = jnp.dot(
+                    a_ref[...], w_ref[:, columns(owner, j)], preferred_element_type=f32
+                ).astype(bf16)
+
+            copy = pltpu.make_async_remote_copy(
+                src_ref=theirs.at[i],
+                dst_ref=got.at[i],
+                send_sem=ps.at[i],
+                recv_sem=pr.at[i],
+                device_id={"tensor": sibling},
+                device_id_type=pl.DeviceIdType.MESH,
+            )
+            copy.start()
+            first.append(copy)
+        for i, d in enumerate(turns):
+            owner = lax.rem(chip + d, chips) * 2 + core
+            first[i].wait_recv()
+
+            @pl.loop(0, width // tile)
+            def _(j, i=i, d=d, owner=owner):
+                own = jnp.dot(
+                    a_ref[...], w_ref[:, columns(owner, j)], preferred_element_type=f32
+                )
+                pair = own + got[i, :, here(j)].astype(f32)
+                if d == 0:
+                    acc[:, here(j)] = pair
+                else:
+                    merged[i, :, here(j)] = pair.astype(bf16)
+
+            if d != 0:
+                copy = pltpu.make_async_remote_copy(
+                    src_ref=merged.at[i],
+                    dst_ref=landed.at[i],
+                    send_sem=cs.at[i],
+                    recv_sem=cr.at[i],
+                    device_id={"tensor": owner},
+                    device_id_type=pl.DeviceIdType.MESH,
+                )
+                copy.start()
+                second.append(copy)
+        for copy in second:
+            copy.wait_recv()
+
+        @pl.loop(0, width // tile)
+        def _(j):
+            total = acc[:, here(j)]
+            for i in range(chips - 1):
+                total = total + landed[i, :, here(j)].astype(f32)
+            out_ref[:, here(j)] = total.astype(bf16)
+
+        for copy in first + second:
+            copy.wait_send()
+
+    vmem = pl.BlockSpec(memory_space=pltpu.VMEM)
+    return pl.pallas_call(
+        kernel,
+        out_shape=jax.ShapeDtypeStruct((rows, width), bf16),
+        in_specs=[vmem, vmem],
+        out_specs=vmem,
+        scratch_shapes=[
+            pltpu.VMEM((chips, rows, width), bf16),
+            pltpu.VMEM((chips, rows, width), bf16),
+            pltpu.VMEM((chips - 1, rows, width), bf16),
+            pltpu.VMEM((chips - 1, rows, width), bf16),
+            pltpu.VMEM((rows, width), f32),
+            pltpu.SemaphoreType.DMA((chips,)),
+            pltpu.SemaphoreType.DMA((chips,)),
+            pltpu.SemaphoreType.DMA((chips - 1,)),
+            pltpu.SemaphoreType.DMA((chips - 1,)),
+        ],
+        compiler_params=pltpu.CompilerParams(
+            collective_id=0, has_side_effects=True, vmem_limit_bytes=36 * 1024 * 1024
+        ),
+    )(values, weight)
 
 
 def attend(tables, lengths, moving, spots, cache, landed, queries, fresh, fresh_tokens):
@@ -177,16 +290,17 @@
     pages_out = jnp.sum(jnp.where(hot[:, :, None], block_table[None], 0), axis=1).reshape(-1)
     received = pick_blocks(pages_out, key_value_cache).reshape(MIG_DEV, span, tracks)
     flips = lax.dynamic_slice(partner, (replica_rank, tensor_rank), (1, 1))[0, 0] ^ replica_rank
-    bit = 1
-    while bit < replicas:
+    hops = [1 << i for i in range((replicas - 1).bit_length())]
+
+    def hop(held, bit):
         pairs = [(i, i ^ bit) for i in range(replicas)]
-        other = lax.ppermute(received, "replica", pairs)
-        received = jnp.where((flips & bit) != 0, other, received)
-        bit *= 2
+        other = lax.ppermute(held, "replica", pairs)
+        return jnp.where((flips & bit) != 0, other, held)
 
     local_gain = lax.dynamic_slice_in_dim(
         input_norm_gain, tensor_rank * width_local, width_local, 0
     ).astype(f32)
+    local_gain, received = lax.optimization_barrier((local_gain, received))
     scaled_rows = (all_rows.astype(f32) * local_gain).astype(bf16)
     inner = jnp.einsum(
         "nd,cd->nc",
@@ -202,6 +316,8 @@
         "rc,nc->rn", spread, jnp.where(chosen, inner, 0.0).astype(bf16), preferred_element_type=f32
     ).astype(bf16)
     parts = lax.all_gather(part, "tensor", axis=0)
+    received = hop(received, hops[0])
+    parts, received, gathered = lax.optimization_barrier((parts, received, gathered))
     shrink_low = jnp.sum(parts.astype(f32), axis=0).astype(bf16)
     wide = jnp.einsum("rn,rc->nc", shrink_low, spread, preferred_element_type=f32)
     wide = jnp.where(chosen, wide, 0.0).astype(bf16)
@@ -209,6 +325,9 @@
         wide, adapter_up.reshape(owned * rank, column_local), preferred_element_type=f32
     ).astype(bf16)
     expand = lax.psum_scatter(expand, "replica", scatter_dimension=0, tiled=True)
+    for bit in hops[1:]:
+        received = hop(received, bit)
+    expand, received = lax.optimization_barrier((expand, received))
 
     gathered_f = gathered.astype(f32)
     factor = lax.rsqrt(jnp.mean(gathered_f * gathered_f, axis=-1, keepdims=True) + norm_eps)
@@ -255,8 +374,7 @@
     returned = lax.all_to_all(
         jnp.transpose(attended, (1, 0, 2)), "tensor", split_axis=0, concat_axis=0, tiled=True
     ).reshape(rows, heads_local)
-    partial = jnp.dot(returned, output_weight, preferred_element_type=f32).astype(bf16)
-    summed = lax.psum_scatter(partial, "tensor", scatter_dimension=1, tiled=True)
+    summed = project_out(returned, output_weight, tensors)
 
     hot_f = hot.astype(bf16)
     moved = jnp.einsum(

time: 358 us -> 347 us (0.969)
  waiting for transfers between devices: 200 us -> 179 us
  local copies, waits for them, and re-layouts: 14.2 us -> 26.7 us
  blocking collectives: 22.6 us -> 10.5 us
  matrix products: 30.6 us -> 22.5 us
  starting transfers between devices: 5.6 us -> 13.2 us
  other arithmetic: 10.6 us -> 15.2 us
  Pallas kernels: 59.5 us -> 63.7 us
    ppermute x2, waiting for transfers between devices: 37.9 us -> 137 us  [hop(): other = lax.ppermute(held, 'replica', pairs)]
    reduce_scatter x1 -> x0, waiting for transfers between devices: 55.2 us -> none  [per_device(): lax.psum_scatter(partial, 'tensor', scatter_dimension=1, tiled=True)]
    all_gather x1, waiting for transfers between devices: 55.1 us -> 0.01 us  [per_device(): all_rows = lax.all_gather(hidden, 'replica', axis=0, tiled=True)]
    reduce_scatter x1, waiting for transfers between devices: 45.3 us -> 0.02 us  [per_device(): lax.psum_scatter(expand, 'replica', scatter_dimension=0, tiled=True)]
    pallas_call x0 -> x1, Pallas kernels: none -> 36.5 us  [project_out(): pl.pallas_call(kernel, out_shape=jax.ShapeDtypeStruct((rows, width), bf16...]
    pallas_call x1, Pallas kernels: 33.7 us -> 2.03 us  [pick_blocks(): pl.pallas_call(kernel, out_shape=jax.ShapeDtypeStruct((count,) + cache.sh...]
    all_gather x1, waiting for transfers between devices: 0.02 us -> 26.6 us  [per_device(): gathered = lax.all_gather(hidden, 'tensor', axis=1, tiled=True)]
    all_to_all x1 -> x0, blocking collectives: 11.8 us -> none  [per_device(): lax.all_to_all(jnp.transpose(attended, (1, 0, 2)), 'tensor', split_axis=0...]
  transfers between devices with their start and end apart: 7 -> 7, of which waited for: 5 -> 5; matrix products, arithmetic and copies ran while one was open for 10% -> 6% of each run, Pallas kernels for 9% -> 1%
where the time goes in v2:
time: 347 us; the launch traced here: 346 us
  waiting for transfers between devices  179 us (52%)
  Pallas kernels  63.7 us (18%)
  local copies, waits for them, and re-layouts  26.7 us (8%)
  matrix products  22.5 us (6%)
  other arithmetic  15.2 us (4%)
  between operations  14.7 us (4%)
  starting transfers between devices  13.2 us (4%)
  blocking collectives  10.5 us (3%)
    ppermute x2, waiting for transfers between devices, hop(): other = lax.ppermute(held, 'replica', pairs)  137 us
    pallas_call x1, Pallas kernels, project_out(): pl.pallas_call(kernel, out_shape=jax.ShapeDtypeStruct((rows, width), bf16...  36.5 us
    all_gather x1, waiting for transfers between devices, per_device(): gathered = lax.all_gather(hidden, 'tensor', axis=1, tiled=True)  26.6 us
    pallas_call x1, Pallas kernels, attend(): pl.pallas_call(kernel, out_shape=jax.ShapeDtypeStruct((slots, query_rows,...  25.2 us
    unnamed x25, local copies, waits for them, and re-layouts  11.6 us
    dot_general x1, matrix products, per_device(): base = jnp.dot(scaled, merged_weight, preferred_element_type=f32)  11.1 us
    all_gather x1, blocking collectives, per_device(): parts = lax.all_gather(part, 'tensor', axis=0)  10.5 us
    all_to_all x1, waiting for transfers between devices, per_device(): lax.all_to_all(projected.reshape(tensors, slots * fresh_tokens, column_lo...  8.95 us
  transfers between devices with their start and end apart: 7, of which 5 were waited for; matrix products, arithmetic and copies ran while one was open for 6% of the time, Pallas kernels for 1%

profile of v2, /device:TPU:0, one launch (start us, length us, event | category | flops | bytes accessed | tf_op | source)
XLA Modules:
  0.0 345.6 jit_solution(16475559360064764998)
XLA Ops:
  7.2 0.0 copy-start
  7.2 0.0 all-gather.4.cloned.1.call-start
  7.2 2.9 reshape.238
  10.1 0.0 all-gather.4.cloned.1.call-update
  10.1 0.0 all-gather.6.cloned.1.call-start
  10.2 0.7 all-gather.6.cloned.1.call-update
  10.9 0.0 reduce-scatter.2.cloned.1.call-start
  10.9 0.8 select_reduce_fusion
  11.7 0.7 broadcast_compare_fusion
  12.4 0.8 select_reduce_fusion.2
  13.1 0.8 select_reduce_fusion.1
  14.0 0.1 reshape.239.pages_ref
  14.0 4.0 %copy-done.1 = bf16[160,16,2048]{2,1,0:T(8,128)(2,1)S(1)} copy-done((bf16[160,16,2048]{2,1,0:T(8,128)(2,1)S(1)}, bf16[160,16,2048]{2,1,0:T(8,128)(2,1)}, u32[]{:S(2)}) %copy-start.1) | copy-done | bytes 10485784
  18.0 2.0 shard_map.131
  20.1 3.1 collective-permute-start
  23.2 1.3 dynamic_slice.7
  25.1 0.1 broadcast_in_dim.134
  25.3 0.2 eq.92
  25.5 62.7 %collective-permute-done = bf16[2,128,2048]{2,1,0:T(8,128)(2,1)} collective-permute-done((bf16[2,128,2048]{2,1,0:T(8,128)(2,1)S(1)}, bf16[2,128,2048]{2,1,0:T(8,128)(2,1)}, u32[]{:S(2)}, u32[]{:S(2)}) %collective-permute-start) | collective-permute-done | bytes 1048608 | tf_op jit(solution)/shard_map/ppermute | solution.py:297
  88.2 2.3 broadcast_select_fusion.1
  90.6 5.3 %convolution_convert_fusion.2 = bf16[16,1280]{1,0:T(8,128)(2,1)S(1)} fusion(bf16[1024,1024]{1,0:T(8,128)(2,1)S(1)} %bitcast.36, bf16[1280,1024]{1,0:T(8,128)(2,1)} %all-gather.4.cloned.1.call-done, f32[1024]{0:T(1024)S(1)} %dynamic-slice_convert_fusion, s32[1024]{0:T(1024)S(1)} %get-tuple-element.29, s32[1280]{0:T(1024)S(1)} %eq.92, ...), kind=kOutput, calls=%fused_computation.14 | convolution fusion | flops 2734198784 | bytes 4776960 | tf_op jit(solution)/shard_map/rc,nc->rn/dot_general | solution.py:315
  95.9 10.5 %all-gather = bf16[128,1280]{1,0:T(8,128)(2,1)S(1)} all-gather(bf16[16,1280]{1,0:T(8,128)(2,1)S(1)} %convolution_convert_fusion.2), channel_id=2, replica_groups=mesh['replica'=4,'tensor'=8] {'tensor'}, dimensions={0}, use_global_device_ids=true | all-gather | bytes 368640 | tf_op jit(solution)/shard_map/all_gather | solution.py:318
  106.4 26.6 %all-gather.6.cloned.1.call-done = bf16[320,8192]{1,0:T(8,128)(2,1)} async-done(((bf16[320,1024]{1,0:T(8,128)(2,1)}), bf16[320,8192]{1,0:T(8,128)(2,1)}) %all-gather.6.cloned.1.call-update) | async-done | bytes 5242896 | tf_op jit(solution)/shard_map/all_gather | solution.py:282
  133.0 0.0 copy-start.9
  133.0 0.0 copy-start.4
  133.0 5.9 %convolution_convert_fusion.1 = bf16[1280,768]{1,0:T(8,128)(2,1)} fusion(bf16[1024,768]{1,0:T(8,128)(2,1)} %bitcast.50, bf16[16,1280]{1,0:T(8,128)(2,1)S(1)} %reduce_sum.50, s32[1024]{0:T(1024)S(1)} %get-tuple-element.29, s32[1280]{0:T(1024)S(1)} %eq.92, s32[1024]{0:T(1024)S(1)} %get-tuple-element.28), kind=kOutput, calls=%fused_computation.12 | convolution fusion | flops 2060140544 | bytes 3593216 | tf_op jit(solution)/shard_map/dot_general | solution.py:324
  138.9 0.0 reduce-scatter.2.cloned.1.call-update
  139.0 0.1 iota_compare_fusion.6
  139.0 2.4 collective-permute-start.1
  141.5 0.1 copy.27
  141.6 0.1 reduce_or.9
  141.7 0.1 reshape.237.tab
  141.8 0.1 add_convert_fusion
  141.9 3.7 %fusion = f32[320]{0:T(512)S(1)} fusion(bf16[320,8192]{1,0:T(8,128)(2,1)} %all-gather.6.cloned.1.call-done), kind=kLoop, calls=%fused_computation.2 | loop fusion | flops 7864000 | bytes 5244160 | tf_op jit(solution)/shard_map/reduce_sum | solution.py:333
  145.6 73.9 %collective-permute-done.1 = bf16[2,128,2048]{2,1,0:T(8,128)(2,1)} collective-permute-done((bf16[2,128,2048]{2,1,0:T(8,128)(2,1)S(1)}, bf16[2,128,2048]{2,1,0:T(8,128)(2,1)}, u32[]{:S(2)}, u32[]{:S(2)}) %collective-permute-start.1) | collective-permute-done | bytes 1048608 | tf_op jit(solution)/shard_map/ppermute | solution.py:297
  219.5 1.3 broadcast_select_fusion.landed_ref
  220.8 0.0 reduce-scatter.2.cloned.1.call-done
  220.8 11.1 %fusion.14 = bf16[320,768]{1,0:T(8,128)(2,1)} fusion(bf16[8192,768]{1,0:T(8,128)(2,1)} %param.14, bf16[320,8192]{1,0:T(8,128)(2,1)} %all-gather.6.cloned.1.call-done, f32[8192]{0:T(1024)S(1)} %convert_element_type.78, bf16[320,768]{1,0:T(8,128)(2,1)} %reduce-scatter.2.cloned.1.call-done, f32[320]{0:T(512)S(1)} %add_rsqrt_fusion), kind=kOutput, calls=%fused_computation.17 | convolution fusion | flops 4035624960 | bytes 18842880 | tf_op jit(solution)/shard_map/dot_general | solution.py:335
  231.9 4.1 %all-to-all-start = ((bf16[8,40,768]{2,1,0:T(8,128)(2,1)}), bf16[8,40,768]{2,1,0:T(8,128)(2,1)}, u32[]{:S(2)}, u32[]{:S(2)}) async-start(bf16[8,40,768]{2,1,0:T(8,128)(2,1)} %bitcast.48), calls=%async_computation.1 | async-start | bytes 983040 | tf_op jit(solution)/shard_map/all_to_all | solution.py:338
  236.1 0.1 iota_compare_fusion.7
  236.2 0.4 multiply_cosine_fusion
  236.6 9.0 %all-to-all-done = bf16[8,40,768]{2,1,0:T(8,128)(2,1)} async-done(((bf16[8,40,768]{2,1,0:T(8,128)(2,1)}), bf16[8,40,768]{2,1,0:T(8,128)(2,1)}, u32[]{:S(2)}, u32[]{:S(2)}) %all-to-all-start) | async-done | bytes 491552 | tf_op jit(solution)/shard_map/all_to_all | solution.py:338
  245.5 1.9 copy.28
  247.4 2.2 reshape.244
  249.6 0.9 slice.35
  250.5 1.6 fusion.20
  252.1 1.0 fusion.22
  253.1 0.1 fusion.23
  253.3 0.1 copy.33
  253.4 0.2 convolution_convert_fusion
  253.6 0.2 pad.4.fresh_ref
  253.8 1.2 copy.29
  255.0 0.0 copy-start.2
  255.0 4.0 %copy-done.2 = bf16[160,16,2048]{2,1,0:T(8,128)(2,1)S(1)} copy-done((bf16[160,16,2048]{2,1,0:T(8,128)(2,1)S(1)}, bf16[160,16,2048]{2,1,0:T(8,128)(2,1)}, u32[]{:S(2)}) %copy-start.2) | copy-done | bytes 10485784
  259.0 25.2 %shard_map.132 = bf16[20,64,128]{2,1,0:T(8,128)(2,1)S(1)} custom-call(s32[160]{0:T(256)S(1)} %reshape.237.tab, s32[20]{0:T(128)S(1)} %copy-done.4, s32[20]{0:T(128)S(1)} %copy-done.5, s32[20]{0:T(128)S(1)} %get-tuple-element.27.spot, bf16[160,16,2048]{2,1,0:T(8,128)(2,1)S(1)} %copy-done.2, bf16[2,128,2048]{2,1,0:T(8,128)(2,1)S(1)} %broadcast_select_fusion.landed_ref, ...), custom_call_target="tpu_custom_call" | custom-call | tf_op jit(solution)/shard_map/pallas_call | solution.py:239
  284.2 0.8 reshape.246
  285.0 1.2 copy.30
  286.2 0.8 reshape.247
  287.1 3.4 all-to-all-start.1
  290.5 1.3 select_select_fusion
  291.8 6.3 %all-to-all-done.1 = bf16[8,40,512]{2,1,0:T(8,128)(2,1)S(1)} async-done(((bf16[8,40,512]{2,1,0:T(8,128)(2,1)}), bf16[8,40,512]{2,1,0:T(8,128)(2,1)S(1)}, u32[]{:S(2)}, u32[]{:S(2)}) %all-to-all-start.1) | async-done | bytes 327712 | tf_op jit(solution)/shard_map/all_to_all | solution.py:374
  298.1 3.4 copy-done.3
  301.5 36.5 %shard_map.133 = bf16[320,1024]{1,0:T(8,128)(2,1)S(1)} custom-call(bf16[320,512]{1,0:T(8,128)(2,1)S(1)} %bitcast.40, bf16[512,8192]{1,0:T(8,128)(2,1)S(1)} %copy-done.3), custom_call_target="tpu_custom_call" | custom-call | tf_op jit(solution)/shard_map/pallas_call | solution.py:148
  338.0 1.1 reshape.249
  (28 shorter events, 0.2 us)
Async XLA Ops:
  7.2 83.4 %copy-start = (bf16[64,16,1024]{2,1,0:T(8,128)(2,1)S(1)}, bf16[64,16,1024]{2,1,0:T(8,128)(2,1)}, u32[]{:S(2)}) copy-start(bf16[64,16,1024]{2,1,0:T(8,128)(2,1)} %param.16) | copy-start | bytes 6291460
  7.2 83.4 %all-gather.4.cloned.1.call-start = ((), (), s32[]{:S(2)}) async-start(), calls=%async_computation.3 | async-start | bytes 3276800 | tf_op jit(solution)/shard_map/all_gather | solution.py:281
  10.1 122.8 %all-gather.6.cloned.1.call-start = ((), (), s32[]{:S(2)}) async-start(), calls=%async_computation.4 | async-start | bytes 5898240 | tf_op jit(solution)/shard_map/all_gather | solution.py:282
  10.9 210.0 %reduce-scatter.2.cloned.1.call-start = ((), (), s32[]{:S(2)}) async-start(), calls=%async_computation.5 | async-start | bytes 2457600 | tf_op jit(solution)/shard_map/reduce_scatter | solution.py:327
  14.0 4.0 %copy-start.1 = (bf16[160,16,2048]{2,1,0:T(8,128)(2,1)S(1)}, bf16[160,16,2048]{2,1,0:T(8,128)(2,1)}, u32[]{:S(2)}) copy-start(bf16[160,16,2048]{2,1,0:T(8,128)(2,1)} %cache_ref.3) | copy-start | bytes 31457284
  18.0 2.0 copy-start.8
  18.0 7.1 %copy-start.10 = (s32[640]{0:T(1024)S(1)}, s32[640]{0:T(1024)}, u32[]{:S(2)}) copy-start(s32[640]{0:T(1024)} %param.18) | copy-start | bytes 7684
  20.1 68.1 %collective-permute-start = (bf16[2,128,2048]{2,1,0:T(8,128)(2,1)S(1)}, bf16[2,128,2048]{2,1,0:T(8,128)(2,1)}, u32[]{:S(2)}, u32[]{:S(2)}) collective-permute-start(bf16[2,128,2048]{2,1,0:T(8,128)(2,1)S(1)} %bitcast.37), channel_id=1, source_target_pairs={{0,8},{8,0},{16,24},{24,16},{1,9},{9,1},{17,25},{25,17},{2,10},{10... | collective-permute-start | bytes 3145736 | tf_op jit(solution)/shard_map/ppermute | solution.py:297
  133.0 6.0 %copy-start.6 = (bf16[2,128,2048]{2,1,0:T(8,128)(2,1)S(1)}, bf16[2,128,2048]{2,1,0:T(8,128)(2,1)}, u32[]{:S(2)}) copy-start(bf16[2,128,2048]{2,1,0:T(8,128)(2,1)} %broadcast_select_fusion.1) | copy-start | bytes 3145732
  133.0 8.5 %copy-start.9 = (s32[20,8]{0,1:T(8,128)S(1)}, s32[20,8]{0,1:T(8,128)}, u32[]{:S(2)}) copy-start(s32[20,8]{0,1:T(8,128)} %param.20) | copy-start | bytes 1924
  133.0 8.8 %copy-start.4 = (s32[20]{0:T(128)S(1)}, s32[20]{0:T(128)}, u32[]{:S(2)}) copy-start(s32[20]{0:T(128)} %lens.1) | copy-start | bytes 244
  139.0 80.4 %collective-permute-start.1 = (bf16[2,128,2048]{2,1,0:T(8,128)(2,1)S(1)}, bf16[2,128,2048]{2,1,0:T(8,128)(2,1)}, u32[]{:S(2)}, u32[]{:S(2)}) collective-permute-start(bf16[2,128,2048]{2,1,0:T(8,128)(2,1)S(1)} %copy-done.6), channel_id=1, source_target_pairs={{0,16},{8,24},{16,0},{24,8},{1,17},{9,25},{17,1},{25,9},{2,18},{10... | collective-permute-start | bytes 3145736 | tf_op jit(solution)/shard_map/ppermute | solution.py:297
  141.8 77.7 %copy-start.7 = (bf16[2,128,2048]{2,1,0:T(8,128)(2,1)S(1)}, bf16[2,128,2048]{2,1,0:T(8,128)(2,1)}, u32[]{:S(2)}) copy-start(bf16[2,128,2048]{2,1,0:T(8,128)(2,1)} %broadcast_select_fusion.1) | copy-start | bytes 3145732
  231.9 13.6 %all-to-all-start = ((bf16[8,40,768]{2,1,0:T(8,128)(2,1)}), bf16[8,40,768]{2,1,0:T(8,128)(2,1)}, u32[]{:S(2)}, u32[]{:S(2)}) async-start(bf16[8,40,768]{2,1,0:T(8,128)(2,1)} %bitcast.48), calls=%async_computation.1 | async-start | bytes 983040 | tf_op jit(solution)/shard_map/all_to_all | solution.py:338
  236.5 18.5 %copy-start.5 = (s32[20]{0:T(128)S(1)}, s32[20]{0:T(128)}, u32[]{:S(2)}) copy-start(s32[20]{0:T(128)} %mov.1) | copy-start | bytes 244
  255.0 4.0 %copy-start.2 = (bf16[160,16,2048]{2,1,0:T(8,128)(2,1)S(1)}, bf16[160,16,2048]{2,1,0:T(8,128)(2,1)}, u32[]{:S(2)}) copy-start(bf16[160,16,2048]{2,1,0:T(8,128)(2,1)} %cache_ref.3) | copy-start | bytes 31457284
  287.1 11.0 %all-to-all-start.1 = ((bf16[8,40,512]{2,1,0:T(8,128)(2,1)}), bf16[8,40,512]{2,1,0:T(8,128)(2,1)S(1)}, u32[]{:S(2)}, u32[]{:S(2)}) async-start(bf16[8,40,512]{2,1,0:T(8,128)(2,1)} %bitcast.43), calls=%async_computation.2 | async-start | bytes 655360 | tf_op jit(solution)/shard_map/all_to_all | solution.py:374
  298.1 3.4 copy-start.3
Sparse Core Ops, SparseCore 0:
  10.2 76.6 all-gather.3
  89.4 43.5 all-gather.5
  139.1 69.4 reduce-scatter.1

commit v3 on v2

--- a/solution.py
+++ b/solution.py
@@ -162,7 +162,7 @@
             pltpu.SemaphoreType.DMA((chips - 1,)),
         ],
         compiler_params=pltpu.CompilerParams(
-            collective_id=0, has_side_effects=True, vmem_limit_bytes=36 * 1024 * 1024
+            collective_id=0, has_side_effects=True, vmem_limit_bytes=30 * 1024 * 1024
         ),
     )(values, weight)
 
@@ -245,7 +245,7 @@
             pltpu.VMEM((slots, total, tracks), jnp.bfloat16),
             pltpu.SemaphoreType.DMA((slots,)),
         ],
-        compiler_params=pltpu.CompilerParams(vmem_limit_bytes=40 * 1024 * 1024),
+        compiler_params=pltpu.CompilerParams(vmem_limit_bytes=22 * 1024 * 1024),
     )(tables, lengths, moving, spots, cache, landed, queries, fresh)
 
 
@@ -300,7 +300,7 @@
     local_gain = lax.dynamic_slice_in_dim(
         input_norm_gain, tensor_rank * width_local, width_local, 0
     ).astype(f32)
-    local_gain, received = lax.optimization_barrier((local_gain, received))
+    all_rows, received = lax.optimization_barrier((all_rows, received))
     scaled_rows = (all_rows.astype(f32) * local_gain).astype(bf16)
     inner = jnp.einsum(
         "nd,cd->nc",
@@ -316,7 +316,8 @@
         "rc,nc->rn", spread, jnp.where(chosen, inner, 0.0).astype(bf16), preferred_element_type=f32
     ).astype(bf16)
     parts = lax.all_gather(part, "tensor", axis=0)
-    received = hop(received, hops[0])
+    for bit in hops:
+        received = hop(received, bit)
     parts, received, gathered = lax.optimization_barrier((parts, received, gathered))
     shrink_low = jnp.sum(parts.astype(f32), axis=0).astype(bf16)
     wide = jnp.einsum("rn,rc->nc", shrink_low, spread, preferred_element_type=f32)
@@ -325,9 +326,6 @@
         wide, adapter_up.reshape(owned * rank, column_local), preferred_element_type=f32
     ).astype(bf16)
     expand = lax.psum_scatter(expand, "replica", scatter_dimension=0, tiled=True)
-    for bit in hops[1:]:
-        received = hop(received, bit)
-    expand, received = lax.optimization_barrier((expand, received))
 
     gathered_f = gathered.astype(f32)
     factor = lax.rsqrt(jnp.mean(gathered_f * gathered_f, axis=-1, keepdims=True) + norm_eps)

time: 347 us -> 317 us (0.914)
  waiting for transfers between devices: 179 us -> 154 us
  starting transfers between devices: 13.2 us -> 8.98 us
    ppermute x2, waiting for transfers between devices: 137 us -> 52.5 us  [hop(): other = lax.ppermute(held, 'replica', pairs)]
    all_gather x1, waiting for transfers between devices: 0.01 us -> 47.1 us  [per_device(): all_rows = lax.all_gather(hidden, 'replica', axis=0, tiled=True)]
    reduce_scatter x1, waiting for transfers between devices: 0.02 us -> 37.9 us  [per_device(): lax.psum_scatter(expand, 'replica', scatter_dimension=0, tiled=True)]
    all_gather x1, waiting for transfers between devices: 26.6 us -> 0.02 us  [per_device(): gathered = lax.all_gather(hidden, 'tensor', axis=1, tiled=True)]
    ppermute x2, starting transfers between devices: 5.51 us -> 1.3 us  [hop(): other = lax.ppermute(held, 'replica', pairs)]
    unnamed x25 -> x23, local copies, waits for them, and re-layouts: 11.6 us -> 11.6 us
  transfers between devices with their start and end apart: 7 -> 7, of which waited for: 5 -> 6; matrix products, arithmetic and copies ran while one was open for 6% -> 6% of each run, Pallas kernels for 1% -> 1%
where the time goes in v3:
time: 317 us; the launch traced here: 316 us
  waiting for transfers between devices  154 us (49%)
  Pallas kernels  63.7 us (20%)
  local copies, waits for them, and re-layouts  26.7 us (8%)
  matrix products  22.4 us (7%)
  other arithmetic  15.7 us (5%)
  between operations  14.7 us (5%)
  blocking collectives  9.99 us (3%)
  starting transfers between devices  8.98 us (3%)
    ppermute x2, waiting for transfers between devices, hop(): other = lax.ppermute(held, 'replica', pairs)  52.5 us
    all_gather x1, waiting for transfers between devices, per_device(): all_rows = lax.all_gather(hidden, 'replica', axis=0, tiled=True)  47.1 us
    reduce_scatter x1, waiting for transfers between devices, per_device(): lax.psum_scatter(expand, 'replica', scatter_dimension=0, tiled=True)  37.9 us
    pallas_call x1, Pallas kernels, project_out(): pl.pallas_call(kernel, out_shape=jax.ShapeDtypeStruct((rows, width), bf16...  36.5 us
    pallas_call x1, Pallas kernels, attend(): pl.pallas_call(kernel, out_shape=jax.ShapeDtypeStruct((slots, query_rows,...  25.2 us
    unnamed x23, local copies, waits for them, and re-layouts  11.6 us
    dot_general x1, matrix products, per_device(): base = jnp.dot(scaled, merged_weight, preferred_element_type=f32)  11.1 us
    all_gather x1, blocking collectives, per_device(): parts = lax.all_gather(part, 'tensor', axis=0)  9.99 us
  transfers between devices with their start and end apart: 7, of which 6 were waited for; matrix products, arithmetic and copies ran while one was open for 6% of the time, Pallas kernels for 1%

profile of v3, /device:TPU:0, one launch (start us, length us, event | category | flops | bytes accessed | tf_op | source)
XLA Modules:
  0.0 315.7 jit_solution(9915725022530454392)
XLA Ops:
  7.2 0.0 copy-start
  7.2 0.0 all-gather.4.cloned.1.call-start
  7.2 2.9 reshape.238
  10.1 0.0 all-gather.4.cloned.1.call-update
  10.1 0.0 all-gather.6.cloned.1.call-start
  10.2 0.7 all-gather.6.cloned.1.call-update
  10.9 0.0 reduce-scatter.2.cloned.1.call-start
  10.9 0.8 select_reduce_fusion
  11.7 0.7 broadcast_compare_fusion
  12.3 1.3 select_reduce_fusion.2
  13.7 0.8 select_reduce_fusion.1
  14.5 0.1 reshape.239.pages_ref
  14.6 4.0 %copy-done.1 = bf16[160,16,2048]{2,1,0:T(8,128)(2,1)S(1)} copy-done((bf16[160,16,2048]{2,1,0:T(8,128)(2,1)S(1)}, bf16[160,16,2048]{2,1,0:T(8,128)(2,1)}, u32[]{:S(2)}) %copy-start.1) | copy-done | bytes 10485784
  18.6 2.0 shard_map.131
  20.6 47.1 %all-gather.4.cloned.1.call-done = bf16[1280,1024]{1,0:T(8,128)(2,1)} async-done(((bf16[320,1024]{1,0:T(8,128)(2,1)}), bf16[1280,1024]{1,0:T(8,128)(2,1)}) %all-gather.4.cloned.1.call-update) | async-done | bytes 2621456 | tf_op jit(solution)/shard_map/all_gather | solution.py:281
  67.8 1.3 dynamic_slice.7
  69.7 23.0 %collective-permute-done = bf16[2,128,2048]{2,1,0:T(8,128)(2,1)} collective-permute-done((bf16[2,128,2048]{2,1,0:T(8,128)(2,1)S(1)}, bf16[2,128,2048]{2,1,0:T(8,128)(2,1)}, u32[]{:S(2)}, u32[]{:S(2)}) %collective-permute-start) | collective-permute-done | bytes 1048608 | tf_op jit(solution)/shard_map/ppermute | solution.py:297
  92.7 2.4 broadcast_select_fusion
  95.1 1.3 collective-permute-start.1
  96.4 0.1 broadcast_in_dim.134
  96.5 0.2 eq.95
  96.8 5.3 %convolution_convert_fusion.2 = bf16[16,1280]{1,0:T(8,128)(2,1)S(1)} fusion(bf16[1024,1024]{1,0:T(8,128)(2,1)S(1)} %bitcast.36, bf16[1280,1024]{1,0:T(8,128)(2,1)} %all-gather.4.cloned.1.call-done, f32[1024]{0:T(1024)S(1)} %dynamic-slice_convert_fusion, s32[1024]{0:T(1024)S(1)} %get-tuple-element.24, s32[1280]{0:T(1024)S(1)} %eq.95, ...), kind=kOutput, calls=%fused_computation.14 | convolution fusion | flops 2734198784 | bytes 4776960 | tf_op jit(solution)/shard_map/rc,nc->rn/dot_general | solution.py:315
  102.1 10.0 %all-gather = bf16[128,1280]{1,0:T(8,128)(2,1)S(1)} all-gather(bf16[16,1280]{1,0:T(8,128)(2,1)S(1)} %convolution_convert_fusion.2), channel_id=2, replica_groups=mesh['replica'=4,'tensor'=8] {'tensor'}, dimensions={0}, use_global_device_ids=true | all-gather | bytes 368640 | tf_op jit(solution)/shard_map/all_gather | solution.py:318
  112.1 29.4 %collective-permute-done.1 = bf16[2,128,2048]{2,1,0:T(8,128)(2,1)} collective-permute-done((bf16[2,128,2048]{2,1,0:T(8,128)(2,1)}, bf16[2,128,2048]{2,1,0:T(8,128)(2,1)}, u32[]{:S(2)}, u32[]{:S(2)}) %collective-permute-start.1) | collective-permute-done | bytes 1048608 | tf_op jit(solution)/shard_map/ppermute | solution.py:297
  141.5 1.3 broadcast_select_fusion.1.landed_ref
  142.9 0.0 all-gather.6.cloned.1.call-done
  143.0 0.0 copy-start.7
  143.0 0.0 copy-start.4
  143.0 5.8 %convolution_convert_fusion.1 = bf16[1280,768]{1,0:T(8,128)(2,1)} fusion(bf16[1024,768]{1,0:T(8,128)(2,1)} %bitcast.50, bf16[16,1280]{1,0:T(8,128)(2,1)S(1)} %reduce_sum.51, s32[1024]{0:T(1024)S(1)} %get-tuple-element.24, s32[1280]{0:T(1024)S(1)} %eq.95, s32[1024]{0:T(1024)S(1)} %get-tuple-element.25), kind=kOutput, calls=%fused_computation.12 | convolution fusion | flops 2060140544 | bytes 3593216 | tf_op jit(solution)/shard_map/dot_general | solution.py:325
  148.8 0.0 reduce-scatter.2.cloned.1.call-update
  148.9 0.1 copy.27
  149.0 0.1 reduce_or.9
  149.1 0.1 reshape.237.tab
  149.2 0.1 iota_compare_fusion.6
  149.3 0.1 add_convert_fusion
  149.4 3.6 %fusion = f32[320]{0:T(512)S(1)} fusion(bf16[320,8192]{1,0:T(8,128)(2,1)} %all-gather.6.cloned.1.call-done), kind=kLoop, calls=%fused_computation.2 | loop fusion | flops 7864000 | bytes 5244160 | tf_op jit(solution)/shard_map/reduce_sum | solution.py:331
  153.0 37.9 %reduce-scatter.2.cloned.1.call-done = bf16[320,768]{1,0:T(8,128)(2,1)} async-done(((bf16[1280,768]{1,0:T(8,128)(2,1)}), bf16[320,768]{1,0:T(8,128)(2,1)}) %reduce-scatter.2.cloned.1.call-update) | async-done | bytes 491536 | tf_op jit(solution)/shard_map/reduce_scatter | solution.py:328
  190.9 11.1 %fusion.14 = bf16[320,768]{1,0:T(8,128)(2,1)} fusion(bf16[8192,768]{1,0:T(8,128)(2,1)} %param.14, bf16[320,8192]{1,0:T(8,128)(2,1)} %all-gather.6.cloned.1.call-done, f32[8192]{0:T(1024)S(1)} %convert_element_type.76, bf16[320,768]{1,0:T(8,128)(2,1)} %reduce-scatter.2.cloned.1.call-done, f32[320]{0:T(512)S(1)} %add_rsqrt_fusion), kind=kOutput, calls=%fused_computation.17 | convolution fusion | flops 4035624960 | bytes 18842880 | tf_op jit(solution)/shard_map/dot_general | solution.py:333
  202.0 4.1 %all-to-all-start = ((bf16[8,40,768]{2,1,0:T(8,128)(2,1)}), bf16[8,40,768]{2,1,0:T(8,128)(2,1)}, u32[]{:S(2)}, u32[]{:S(2)}) async-start(bf16[8,40,768]{2,1,0:T(8,128)(2,1)} %bitcast.48), calls=%async_computation.1 | async-start | bytes 983040 | tf_op jit(solution)/shard_map/all_to_all | solution.py:336
  206.1 0.1 iota_compare_fusion.7
  206.2 0.4 multiply_cosine_fusion
  206.6 9.0 %all-to-all-done = bf16[8,40,768]{2,1,0:T(8,128)(2,1)} async-done(((bf16[8,40,768]{2,1,0:T(8,128)(2,1)}), bf16[8,40,768]{2,1,0:T(8,128)(2,1)}, u32[]{:S(2)}, u32[]{:S(2)}) %all-to-all-start) | async-done | bytes 491552 | tf_op jit(solution)/shard_map/all_to_all | solution.py:336
  215.6 1.9 copy.28
  217.4 2.2 reshape.244
  219.7 0.9 slice.35
  220.6 1.6 fusion.20
  222.2 1.0 fusion.22
  223.2 0.1 fusion.23
  223.4 0.1 copy.33
  223.4 0.2 convolution_convert_fusion
  223.6 0.2 pad.4.fresh_ref
  223.8 1.2 copy.29
  225.1 0.0 copy-start.2
  225.1 4.0 %copy-done.2 = bf16[160,16,2048]{2,1,0:T(8,128)(2,1)S(1)} copy-done((bf16[160,16,2048]{2,1,0:T(8,128)(2,1)S(1)}, bf16[160,16,2048]{2,1,0:T(8,128)(2,1)}, u32[]{:S(2)}) %copy-start.2) | copy-done | bytes 10485784
  229.0 25.2 %shard_map.132 = bf16[20,64,128]{2,1,0:T(8,128)(2,1)S(1)} custom-call(s32[160]{0:T(256)S(1)} %reshape.237.tab, s32[20]{0:T(128)S(1)} %copy-done.4, s32[20]{0:T(128)S(1)} %copy-done.5, s32[20]{0:T(128)S(1)} %get-tuple-element.23.spot, bf16[160,16,2048]{2,1,0:T(8,128)(2,1)S(1)} %copy-done.2, bf16[2,128,2048]{2,1,0:T(8,128)(2,1)S(1)} %broadcast_select_fusion.1.landed_ref, ...), custom_call_target="tpu_custom_call" | custom-call | tf_op jit(solution)/shard_map/pallas_call | solution.py:239
  254.2 0.8 reshape.246
  255.1 1.2 copy.30
  256.3 0.8 reshape.247
  257.1 3.4 %all-to-all-start.1 = ((bf16[8,40,512]{2,1,0:T(8,128)(2,1)}), bf16[8,40,512]{2,1,0:T(8,128)(2,1)S(1)}, u32[]{:S(2)}, u32[]{:S(2)}) async-start(bf16[8,40,512]{2,1,0:T(8,128)(2,1)} %bitcast.43), calls=%async_computation.2 | async-start | bytes 655360 | tf_op jit(solution)/shard_map/all_to_all | solution.py:372
  260.6 1.3 select_select_fusion
  261.8 6.3 %all-to-all-done.1 = bf16[8,40,512]{2,1,0:T(8,128)(2,1)S(1)} async-done(((bf16[8,40,512]{2,1,0:T(8,128)(2,1)}), bf16[8,40,512]{2,1,0:T(8,128)(2,1)S(1)}, u32[]{:S(2)}, u32[]{:S(2)}) %all-to-all-start.1) | async-done | bytes 327712 | tf_op jit(solution)/shard_map/all_to_all | solution.py:372
  268.1 3.4 %copy-done.3 = bf16[512,8192]{1,0:T(8,128)(2,1)S(1)} copy-done((bf16[512,8192]{1,0:T(8,128)(2,1)S(1)}, bf16[512,8192]{1,0:T(8,128)(2,1)}, u32[]{:S(2)}) %copy-start.3) | copy-done | bytes 8388632
  271.5 36.5 %shard_map.133 = bf16[320,1024]{1,0:T(8,128)(2,1)S(1)} custom-call(bf16[320,512]{1,0:T(8,128)(2,1)S(1)} %bitcast.40, bf16[512,8192]{1,0:T(8,128)(2,1)S(1)} %copy-done.3), custom_call_target="tpu_custom_call" | custom-call | tf_op jit(solution)/shard_map/pallas_call | solution.py:148
  308.1 1.1 reshape.249
  (26 shorter events, 0.2 us)
Async XLA Ops:
  7.2 89.6 %copy-start = (bf16[64,16,1024]{2,1,0:T(8,128)(2,1)S(1)}, bf16[64,16,1024]{2,1,0:T(8,128)(2,1)}, u32[]{:S(2)}) copy-start(bf16[64,16,1024]{2,1,0:T(8,128)(2,1)} %param.16) | copy-start | bytes 6291460
  7.2 60.6 %all-gather.4.cloned.1.call-start = ((), (), s32[]{:S(2)}) async-start(), calls=%async_computation.3 | async-start | bytes 3276800 | tf_op jit(solution)/shard_map/all_gather | solution.py:281
  10.1 132.8 %all-gather.6.cloned.1.call-start = ((), (), s32[]{:S(2)}) async-start(), calls=%async_computation.4 | async-start | bytes 5898240 | tf_op jit(solution)/shard_map/all_gather | solution.py:282
  10.9 180.0 %reduce-scatter.2.cloned.1.call-start = ((), (), s32[]{:S(2)}) async-start(), calls=%async_computation.5 | async-start | bytes 2457600 | tf_op jit(solution)/shard_map/reduce_scatter | solution.py:328
  14.6 4.0 %copy-start.1 = (bf16[160,16,2048]{2,1,0:T(8,128)(2,1)S(1)}, bf16[160,16,2048]{2,1,0:T(8,128)(2,1)}, u32[]{:S(2)}) copy-start(bf16[160,16,2048]{2,1,0:T(8,128)(2,1)} %cache_ref.3) | copy-start | bytes 31457284
  18.6 77.8 %copy-start.8 = (s32[640]{0:T(1024)S(1)}, s32[640]{0:T(1024)}, u32[]{:S(2)}) copy-start(s32[640]{0:T(1024)} %param.18) | copy-start | bytes 7684
  18.6 78.2 %copy-start.6 = (bf16[8192]{0:T(1024)(128)(2,1)S(1)}, bf16[8192]{0:T(1024)(128)(2,1)}, u32[]{:S(2)}) copy-start(bf16[8192]{0:T(1024)(128)(2,1)} %param.13) | copy-start | bytes 49156
  67.8 25.0 %collective-permute-start = (bf16[2,128,2048]{2,1,0:T(8,128)(2,1)S(1)}, bf16[2,128,2048]{2,1,0:T(8,128)(2,1)}, u32[]{:S(2)}, u32[]{:S(2)}) collective-permute-start(bf16[2,128,2048]{2,1,0:T(8,128)(2,1)S(1)} %bitcast.37), channel_id=1, source_target_pairs={{0,8},{8,0},{16,24},{24,16},{1,9},{9,1},{17,25},{25,17},{2,10},{10... | collective-permute-start | bytes 3145736 | tf_op jit(solution)/shard_map/ppermute | solution.py:297
  95.1 46.4 %collective-permute-start.1 = (bf16[2,128,2048]{2,1,0:T(8,128)(2,1)}, bf16[2,128,2048]{2,1,0:T(8,128)(2,1)}, u32[]{:S(2)}, u32[]{:S(2)}) collective-permute-start(bf16[2,128,2048]{2,1,0:T(8,128)(2,1)} %broadcast_select_fusion), channel_id=1, source_target_pairs={{0,16},{8,24},{16,0},{24,8},{1,17},{9,25},{17,1},{25,9},{2,18},{10... | collective-permute-start | bytes 3145736 | tf_op jit(solution)/shard_map/ppermute | solution.py:297
  143.0 5.9 %copy-start.7 = (s32[20,8]{0,1:T(8,128)S(1)}, s32[20,8]{0,1:T(8,128)}, u32[]{:S(2)}) copy-start(s32[20,8]{0,1:T(8,128)} %param.20) | copy-start | bytes 1924
  143.0 6.2 %copy-start.9 = (s32[2]{0:T(128)S(1)}, s32[2]{0:T(128)}, u32[]{:S(2)}) copy-start(s32[2]{0:T(128)} %get-tuple-element.12) | copy-start | bytes 28
  143.0 6.3 %copy-start.4 = (s32[20]{0:T(128)S(1)}, s32[20]{0:T(128)}, u32[]{:S(2)}) copy-start(s32[20]{0:T(128)} %lens.1) | copy-start | bytes 244
  202.0 13.5 %all-to-all-start = ((bf16[8,40,768]{2,1,0:T(8,128)(2,1)}), bf16[8,40,768]{2,1,0:T(8,128)(2,1)}, u32[]{:S(2)}, u32[]{:S(2)}) async-start(bf16[8,40,768]{2,1,0:T(8,128)(2,1)} %bitcast.48), calls=%async_computation.1 | async-start | bytes 983040 | tf_op jit(solution)/shard_map/all_to_all | solution.py:336
  206.6 18.5 %copy-start.5 = (s32[20]{0:T(128)S(1)}, s32[20]{0:T(128)}, u32[]{:S(2)}) copy-start(s32[20]{0:T(128)} %mov.1) | copy-start | bytes 244
  225.1 4.0 %copy-start.2 = (bf16[160,16,2048]{2,1,0:T(8,128)(2,1)S(1)}, bf16[160,16,2048]{2,1,0:T(8,128)(2,1)}, u32[]{:S(2)}) copy-start(bf16[160,16,2048]{2,1,0:T(8,128)(2,1)} %cache_ref.3) | copy-start | bytes 31457284
  257.1 11.0 %all-to-all-start.1 = ((bf16[8,40,512]{2,1,0:T(8,128)(2,1)}), bf16[8,40,512]{2,1,0:T(8,128)(2,1)S(1)}, u32[]{:S(2)}, u32[]{:S(2)}) async-start(bf16[8,40,512]{2,1,0:T(8,128)(2,1)} %bitcast.43), calls=%async_computation.2 | async-start | bytes 655360 | tf_op jit(solution)/shard_map/all_to_all | solution.py:372
  268.1 3.4 %copy-start.3 = (bf16[512,8192]{1,0:T(8,128)(2,1)S(1)}, bf16[512,8192]{1,0:T(8,128)(2,1)}, u32[]{:S(2)}) copy-start(bf16[512,8192]{1,0:T(8,128)(2,1)} %w_ref.1) | copy-start | bytes 25165828
Sparse Core Ops, SparseCore 0:
  10.2 57.4 all-gather.3
  70.2 40.4 all-gather.5
  149.0 41.8 reduce-scatter.1
